TPU v7x, 512 devices: a whole 4x8x8 slice. The times are simulated.
512 devices in a mesh: tm: 16 (over y, core), freq: 32 (over x, z).
Axes of the slice: x: 4, y: 8, z: 8, core: 2. Of those that a mesh axis runs over, the one named last changes fastest.
Arguments:
- emission: bfloat16 [16, 2, 1048576], P('tm', None, 'freq'), may hold values from 0.05 to 40, as said below
- step_weights: float32 [64, 3], replicated, may hold values from 0.2 to 5
- template_ids: int32 [2], replicated, may hold values from 0 to 63
Outputs:
- posterior: float32 [16, 2, 1048576], P('tm', None, 'freq')
- evidence: float32 [2], replicated
Inputs may be any that keep to these rules, and one draw needn't show every extreme that they name: `emission`: every entry is positive.
All inputs are finite; a program needn't handle non-finite values.
Results may differ from a plain program's by a relative error of at most 0.0003.
Values sent between devices are 32-bit elements; how exact they have to be, the bound alone decides.
A program may use at most 64 MiB of HBM per device.

v0:
```python
import jax
import jax.numpy as jnp
from jax import lax
from jax.sharding import PartitionSpec as P

BINS = 1048576
MBATCH = 2


def extended(block, sides, width):
    for axis, dim in sides:
        count = lax.axis_size(axis)
        forward = [(i, i + 1) for i in range(count - 1)]
        backward = [(target, source) for source, target in forward]
        low = lax.ppermute(
            lax.slice_in_dim(block, block.shape[dim] - width, None, axis=dim), axis, forward
        )
        high = lax.ppermute(lax.slice_in_dim(block, 0, width, axis=dim), axis, backward)
        block = jnp.concatenate([low, block, high], axis=dim)
    return block


def passed_along(array, axis, by):
    peers = lax.axis_size(axis)
    pairs = [(i, i + by) for i in range(peers) if 0 <= i + by < peers]
    return lax.ppermute(array, axis, pairs)


def advance_halo(field, staying, rising, falling):
    padded = extended(field, (("freq", 1),), 1)
    return staying * padded[:, 1:-1] + rising * padded[:, :-2] + falling * padded[:, 2:]


def retreat_halo(field, staying, rising, falling):
    padded = extended(field, (("freq", 1),), 1)
    return staying * padded[:, 1:-1] + rising * padded[:, 2:] + falling * padded[:, :-2]


def forward_block(message, emission_block, staying, rising, falling):

    def forward_one_step(current, emission_row):
        updated = emission_row.astype(jnp.float32) * advance_halo(current, staying, rising, falling)
        growth_step = jnp.zeros((updated.shape[0],), jnp.float32)
        return (updated, (updated, growth_step))

    current, (values, growths) = lax.scan(forward_one_step, message, emission_block)
    return (values, current, jnp.sum(growths, axis=0))


def backward_block(message, emission_block, staying, rising, falling, closing):
    incoming = retreat_halo(message, staying, rising, falling)
    last_field = jnp.where(closing, jnp.ones_like(incoming) / BINS, incoming)

    def backward_one_step(current, emission_row):
        earlier = retreat_halo(emission_row.astype(jnp.float32) * current, staying, rising, falling)
        return (earlier, earlier)

    first_field, earlier_values = lax.scan(
        backward_one_step, last_field, emission_block[1:], reverse=True
    )
    values = jnp.concatenate([earlier_values, last_field[None]], axis=0)
    outgoing = emission_block[0].astype(jnp.float32) * first_field
    return (values, outgoing)


def pass_messages(forward_out, backward_out):
    forward_recv = passed_along(forward_out, "tm", 1)
    backward_recv = passed_along(backward_out, "tm", -1)
    return (forward_recv, backward_recv)


def body(emission, step_weights, template_ids):
    groups = lax.axis_size("tm")
    position = lax.axis_index("tm")
    opening = position == 0
    closing = position == groups - 1
    bank_rows = jnp.arange(step_weights.shape[0], dtype=jnp.int32)
    onehot = (template_ids[:, None] == bank_rows[None, :]).astype(jnp.float32)
    weights = jnp.dot(
        onehot, step_weights, precision=lax.Precision.HIGHEST, preferred_element_type=jnp.float32
    )
    chances = weights / jnp.sum(weights, axis=1, keepdims=True)
    staying, rising, falling = (chances[:, 0:1], chances[:, 1:2], chances[:, 2:3])
    templates = emission.shape[1]
    bins_here = emission.shape[2]
    steps_here = emission.shape[0]
    batch_rows = templates // MBATCH
    uniform = jnp.full((batch_rows, bins_here), 1.0 / BINS, jnp.float32)
    sections = groups + MBATCH - 1

    def take_rows(array, start, axis):
        return lax.dynamic_slice_in_dim(array, start, batch_rows, axis)

    def section_step(section, state_now):
        alphas_now, betas_now, growth_now, forward_out, backward_out = state_now
        forward_recv, backward_recv = pass_messages(forward_out, backward_out)
        forward_in = jnp.where(opening, uniform, forward_recv)
        backward_in = jnp.where(closing, uniform, backward_recv)
        forward_batch = section - position
        backward_batch = section - (groups - 1 - position)
        forward_valid = (forward_batch >= 0) & (forward_batch < MBATCH)
        backward_valid = (backward_batch >= 0) & (backward_batch < MBATCH)
        forward_start = jnp.clip(forward_batch, 0, MBATCH - 1) * batch_rows
        backward_start = jnp.clip(backward_batch, 0, MBATCH - 1) * batch_rows
        new_alphas, new_forward, new_growth = forward_block(
            forward_in,
            take_rows(emission, forward_start, 1),
            take_rows(staying, forward_start, 0),
            take_rows(rising, forward_start, 0),
            take_rows(falling, forward_start, 0),
        )
        new_betas, new_backward = backward_block(
            backward_in,
            take_rows(emission, backward_start, 1),
            take_rows(staying, backward_start, 0),
            take_rows(rising, backward_start, 0),
            take_rows(falling, backward_start, 0),
            closing,
        )
        alphas_now = lax.dynamic_update_slice_in_dim(
            alphas_now,
            jnp.where(forward_valid, new_alphas, take_rows(alphas_now, forward_start, 1)),
            forward_start,
            1,
        )
        growth_now = lax.dynamic_update_slice_in_dim(
            growth_now,
            jnp.where(forward_valid, new_growth, take_rows(growth_now, forward_start, 0)),
            forward_start,
            0,
        )
        betas_now = lax.dynamic_update_slice_in_dim(
            betas_now,
            jnp.where(backward_valid, new_betas, take_rows(betas_now, backward_start, 1)),
            backward_start,
            1,
        )
        return (alphas_now, betas_now, growth_now, new_forward, new_backward)

    empty_fields = jnp.zeros((steps_here, templates, bins_here), jnp.float32)
    start_state = (
        empty_fields,
        empty_fields,
        jnp.zeros((templates,), jnp.float32),
        uniform,
        uniform,
    )
    alphas, betas, growth, _, _ = lax.fori_loop(0, sections, section_step, start_state)
    joint_mass = alphas * betas
    members = (jnp.sum(joint_mass, axis=2), jnp.sum(alphas, axis=2))
    totals = lax.psum((members[0], members[1]), "freq")
    joint_totals = totals[0]
    posterior = BINS * joint_mass / joint_totals[:, :, None]
    growth = jnp.where(closing, jnp.log(totals[1][-1]), jnp.zeros_like(growth))
    evidence = lax.psum(growth, "tm") / (groups * steps_here)
    return (posterior, evidence)


def solution(mesh):
    return jax.shard_map(
        body,
        mesh=mesh,
        in_specs=(P("tm", None, "freq"), P(), P()),
        out_specs=(P("tm", None, "freq"), P()),
        check_vma=False,
    )
```

profile of v0, /device:TPU:1, one launch (start us, length us, event | category | flops | bytes accessed | tf_op | source)
XLA Modules:
  0.0 681.2 jit_solution(15679536397014350551)
XLA Ops:
  3.0 568.1 %while.32 = (s32[]{:T(128)}, f32[1,2,32768]{2,1,0:T(2,128)S(1)}, f32[1,2,32768]{2,1,0:T(2,128)S(1)}, f32[1,32768]{1,0:T(1,128)S(1)}, f32[1,32768]{1,0:T(1,128)S(...) while((s32[]{:T(128)}, f32[1,2,32768]{2,1,0:T(2,128)S(1)}, ...), condition=%wide.region_2.3_spmd.clone, body=%wide.region_1.2_spmd.clone.sunk | while | flops 819215 | bytes 4063971 | solution.py:148
  3.2 4.6 collective-permute-start
  7.9 5.5 collective-permute-start.3
  16.7 4.5 collective-permute-start.2
  45.0 5.4 collective-permute-start.2
  51.2 5.1 collective-permute-start.4
  68.7 4.2 collective-permute-start
  78.3 5.4 collective-permute-start.2
  84.4 4.4 collective-permute-start.4
  101.2 4.2 collective-permute-start
  110.8 5.4 collective-permute-start.2
  116.9 4.4 collective-permute-start.4
  133.7 4.2 collective-permute-start
  143.3 5.4 collective-permute-start.2
  149.5 4.4 collective-permute-start.4
  166.2 4.2 collective-permute-start
  175.8 5.4 collective-permute-start.2
  182.0 4.4 collective-permute-start.4
  208.3 5.4 collective-permute-start.2
  214.5 5.2 collective-permute-start.4
  241.6 5.4 collective-permute-start.2
  247.7 5.3 collective-permute-start.4
  275.0 5.4 collective-permute-start.2
  281.2 5.3 collective-permute-start.4
  298.8 4.2 collective-permute-start
  308.4 5.4 collective-permute-start.2
  314.6 5.3 collective-permute-start.4
  341.8 5.4 collective-permute-start.2
  348.0 5.3 collective-permute-start.4
  375.2 5.4 collective-permute-start.2
  381.4 5.3 collective-permute-start.4
  399.1 4.8 collective-permute-start
  409.3 5.4 collective-permute-start.2
  415.4 5.0 collective-permute-start.4
  432.8 5.7 collective-permute-start
  443.9 5.4 collective-permute-start.2
  450.0 5.0 collective-permute-start.4
  467.4 5.7 collective-permute-start
  478.5 5.4 collective-permute-start.2
  484.7 5.0 collective-permute-start.4
  502.1 5.7 collective-permute-start
  513.1 5.4 collective-permute-start.2
  519.3 5.0 collective-permute-start.4
  536.7 5.7 collective-permute-start
  547.8 5.4 collective-permute-start.2
  553.9 5.0 collective-permute-start.4
  571.6 59.7 %all-reduce = (f32[2]{0:T(128)S(1)}, f32[1,2]{1,0:T(1,128)S(1)}) all-reduce(f32[2]{0:T(128)S(1)} %get-tuple-element.348, f32[1,2]{1,0:T(1,128)S(1)} %bitcast.39), channel_id=1, replica_groups=mesh['tm'=16,'freq'=32] {'freq'}, use_global_device_ids=true, to_apply=%region_4.5 | all-reduce | flops 4 | bytes 32 | tf_op jit(solution)/shard_map/psum | solution.py:151
  632.2 48.4 %psum.23 = f32[2]{0:T(128)S(1)} all-reduce(f32[2]{0:T(128)S(1)} %fusion.11), channel_id=1, replica_groups=mesh['tm'=16,'freq'=32] {'tm'}, use_global_device_ids=true, to_apply=%region_7.8 | all-reduce | flops 2 | bytes 16 | tf_op jit(solution)/shard_map/psum | solution.py:155
  (400 shorter events, 340.7 us)
Async XLA Ops:
  3.2 11.5 %collective-permute-start = (f32[1,32768]{1,0:T(1,128)S(1)}, f32[1,32768]{1,0:T(1,128)S(1)}, u32[]{:S(2)}, u32[]{:S(2)}) collective-permute-start(f32[1,32768]{1,0:T(1,128)S(1)} %broadcast_select_fusion.15), channel_id=1, source_target_pairs={{0,32},{32,64},{64,96},{96,128},{128,160},{160,192},{192,224},{224... | collective-permute-start | bytes 393224 | tf_op jit(solution)/shard_map/while/body/eval_jaxpr/ppermute | solution.py:26
  7.9 13.3 %collective-permute-start.3 = (f32[1,32768]{1,0:T(1,128)S(1)}, f32[1,32768]{1,0:T(1,128)S(1)}, u32[]{:S(2)}, u32[]{:S(2)}) collective-permute-start(f32[1,32768]{1,0:T(1,128)S(1)} %broadcast_select_fusion.18), channel_id=1, source_target_pairs={{32,0},{64,32},{96,64},{128,96},{160,128},{192,160},{224,192},{256... | collective-permute-start | bytes 393224 | tf_op jit(solution)/shard_map/while/body/eval_jaxpr/ppermute | solution.py:26
  43.8 13.9 %collective-permute-start.1 = (f32[1,1]{1,0:T(1,128)}, f32[1,1]{1,0:T(1,128)}, u32[]{:S(2)}, u32[]{:S(2)}) collective-permute-start(f32[1,1]{1,0:T(1,128)} %get-tuple-element.491), channel_id=1, source_target_pairs={{1,0},{2,1},{3,2},{4,3},{5,4},{6,5},{7,6},{8,7},{9,8},{10,9},{11,1... | collective-permute-start | bytes 20 | tf_op jit(solution)/shard_map/while/body/eval_jaxpr/while/body/eval_jaxpr/ppermute | solution.py:18
  45.0 12.6 %collective-permute-start.2 = (f32[1,1]{1,0:T(1,128)}, f32[1,1]{1,0:T(1,128)}, u32[]{:S(2)}, u32[]{:S(2)}) collective-permute-start(f32[1,1]{1,0:T(1,128)} %get-tuple-element.493), channel_id=1, source_target_pairs={{0,1},{1,2},{2,3},{3,4},{4,5},{5,6},{6,7},{7,8},{8,9},{9,10},{10,1... | collective-permute-start | bytes 20 | tf_op jit(solution)/shard_map/while/body/eval_jaxpr/while/body/eval_jaxpr/ppermute | solution.py:15
  51.2 11.7 %collective-permute-start.4 = (f32[1,1]{1,0:T(1,128)}, f32[1,1]{1,0:T(1,128)}, u32[]{:S(2)}, u32[]{:S(2)}) collective-permute-start(f32[1,1]{1,0:T(1,128)} %get-tuple-element.497), channel_id=1, source_target_pairs={{0,1},{1,2},{2,3},{3,4},{4,5},{5,6},{6,7},{7,8},{8,9},{9,10},{10,1... | collective-permute-start | bytes 20 | tf_op jit(solution)/shard_map/while/body/eval_jaxpr/ppermute | solution.py:15
  77.0 13.1 %collective-permute-start.1 = (f32[1,1]{1,0:T(1,128)}, f32[1,1]{1,0:T(1,128)}, u32[]{:S(2)}, u32[]{:S(2)}) collective-permute-start(f32[1,1]{1,0:T(1,128)} %get-tuple-element.491), channel_id=1, source_target_pairs={{1,0},{2,1},{3,2},{4,3},{5,4},{6,5},{7,6},{8,7},{9,8},{10,9},{11,1... | collective-permute-start | bytes 20 | tf_op jit(solution)/shard_map/while/body/eval_jaxpr/while/body/eval_jaxpr/ppermute | solution.py:18
  78.3 11.9 %collective-permute-start.2 = (f32[1,1]{1,0:T(1,128)}, f32[1,1]{1,0:T(1,128)}, u32[]{:S(2)}, u32[]{:S(2)}) collective-permute-start(f32[1,1]{1,0:T(1,128)} %get-tuple-element.493), channel_id=1, source_target_pairs={{0,1},{1,2},{2,3},{3,4},{4,5},{5,6},{6,7},{7,8},{8,9},{9,10},{10,1... | collective-permute-start | bytes 20 | tf_op jit(solution)/shard_map/while/body/eval_jaxpr/while/body/eval_jaxpr/ppermute | solution.py:15
  84.4 11.0 %collective-permute-start.4 = (f32[1,1]{1,0:T(1,128)}, f32[1,1]{1,0:T(1,128)}, u32[]{:S(2)}, u32[]{:S(2)}) collective-permute-start(f32[1,1]{1,0:T(1,128)} %get-tuple-element.497), channel_id=1, source_target_pairs={{0,1},{1,2},{2,3},{3,4},{4,5},{5,6},{6,7},{7,8},{8,9},{9,10},{10,1... | collective-permute-start | bytes 20 | tf_op jit(solution)/shard_map/while/body/eval_jaxpr/ppermute | solution.py:15
  109.5 13.1 %collective-permute-start.1 = (f32[1,1]{1,0:T(1,128)}, f32[1,1]{1,0:T(1,128)}, u32[]{:S(2)}, u32[]{:S(2)}) collective-permute-start(f32[1,1]{1,0:T(1,128)} %get-tuple-element.491), channel_id=1, source_target_pairs={{1,0},{2,1},{3,2},{4,3},{5,4},{6,5},{7,6},{8,7},{9,8},{10,9},{11,1... | collective-permute-start | bytes 20 | tf_op jit(solution)/shard_map/while/body/eval_jaxpr/while/body/eval_jaxpr/ppermute | solution.py:18
  110.8 11.9 %collective-permute-start.2 = (f32[1,1]{1,0:T(1,128)}, f32[1,1]{1,0:T(1,128)}, u32[]{:S(2)}, u32[]{:S(2)}) collective-permute-start(f32[1,1]{1,0:T(1,128)} %get-tuple-element.493), channel_id=1, source_target_pairs={{0,1},{1,2},{2,3},{3,4},{4,5},{5,6},{6,7},{7,8},{8,9},{9,10},{10,1... | collective-permute-start | bytes 20 | tf_op jit(solution)/shard_map/while/body/eval_jaxpr/while/body/eval_jaxpr/ppermute | solution.py:15
  116.9 11.0 %collective-permute-start.4 = (f32[1,1]{1,0:T(1,128)}, f32[1,1]{1,0:T(1,128)}, u32[]{:S(2)}, u32[]{:S(2)}) collective-permute-start(f32[1,1]{1,0:T(1,128)} %get-tuple-element.497), channel_id=1, source_target_pairs={{0,1},{1,2},{2,3},{3,4},{4,5},{5,6},{6,7},{7,8},{8,9},{9,10},{10,1... | collective-permute-start | bytes 20 | tf_op jit(solution)/shard_map/while/body/eval_jaxpr/ppermute | solution.py:15
  142.0 13.1 %collective-permute-start.1 = (f32[1,1]{1,0:T(1,128)}, f32[1,1]{1,0:T(1,128)}, u32[]{:S(2)}, u32[]{:S(2)}) collective-permute-start(f32[1,1]{1,0:T(1,128)} %get-tuple-element.491), channel_id=1, source_target_pairs={{1,0},{2,1},{3,2},{4,3},{5,4},{6,5},{7,6},{8,7},{9,8},{10,9},{11,1... | collective-permute-start | bytes 20 | tf_op jit(solution)/shard_map/while/body/eval_jaxpr/while/body/eval_jaxpr/ppermute | solution.py:18
  143.3 11.9 %collective-permute-start.2 = (f32[1,1]{1,0:T(1,128)}, f32[1,1]{1,0:T(1,128)}, u32[]{:S(2)}, u32[]{:S(2)}) collective-permute-start(f32[1,1]{1,0:T(1,128)} %get-tuple-element.493), channel_id=1, source_target_pairs={{0,1},{1,2},{2,3},{3,4},{4,5},{5,6},{6,7},{7,8},{8,9},{9,10},{10,1... | collective-permute-start | bytes 20 | tf_op jit(solution)/shard_map/while/body/eval_jaxpr/while/body/eval_jaxpr/ppermute | solution.py:15
  174.5 13.1 %collective-permute-start.1 = (f32[1,1]{1,0:T(1,128)}, f32[1,1]{1,0:T(1,128)}, u32[]{:S(2)}, u32[]{:S(2)}) collective-permute-start(f32[1,1]{1,0:T(1,128)} %get-tuple-element.491), channel_id=1, source_target_pairs={{1,0},{2,1},{3,2},{4,3},{5,4},{6,5},{7,6},{8,7},{9,8},{10,9},{11,1... | collective-permute-start | bytes 20 | tf_op jit(solution)/shard_map/while/body/eval_jaxpr/while/body/eval_jaxpr/ppermute | solution.py:18
  175.8 11.9 %collective-permute-start.2 = (f32[1,1]{1,0:T(1,128)}, f32[1,1]{1,0:T(1,128)}, u32[]{:S(2)}, u32[]{:S(2)}) collective-permute-start(f32[1,1]{1,0:T(1,128)} %get-tuple-element.493), channel_id=1, source_target_pairs={{0,1},{1,2},{2,3},{3,4},{4,5},{5,6},{6,7},{7,8},{8,9},{9,10},{10,1... | collective-permute-start | bytes 20 | tf_op jit(solution)/shard_map/while/body/eval_jaxpr/while/body/eval_jaxpr/ppermute | solution.py:15
  207.0 13.9 %collective-permute-start.1 = (f32[1,1]{1,0:T(1,128)}, f32[1,1]{1,0:T(1,128)}, u32[]{:S(2)}, u32[]{:S(2)}) collective-permute-start(f32[1,1]{1,0:T(1,128)} %get-tuple-element.491), channel_id=1, source_target_pairs={{1,0},{2,1},{3,2},{4,3},{5,4},{6,5},{7,6},{8,7},{9,8},{10,9},{11,1... | collective-permute-start | bytes 20 | tf_op jit(solution)/shard_map/while/body/eval_jaxpr/while/body/eval_jaxpr/ppermute | solution.py:18
  208.3 12.6 %collective-permute-start.2 = (f32[1,1]{1,0:T(1,128)}, f32[1,1]{1,0:T(1,128)}, u32[]{:S(2)}, u32[]{:S(2)}) collective-permute-start(f32[1,1]{1,0:T(1,128)} %get-tuple-element.493), channel_id=1, source_target_pairs={{0,1},{1,2},{2,3},{3,4},{4,5},{5,6},{6,7},{7,8},{8,9},{9,10},{10,1... | collective-permute-start | bytes 20 | tf_op jit(solution)/shard_map/while/body/eval_jaxpr/while/body/eval_jaxpr/ppermute | solution.py:15
  214.5 11.7 %collective-permute-start.4 = (f32[1,1]{1,0:T(1,128)}, f32[1,1]{1,0:T(1,128)}, u32[]{:S(2)}, u32[]{:S(2)}) collective-permute-start(f32[1,1]{1,0:T(1,128)} %get-tuple-element.497), channel_id=1, source_target_pairs={{0,1},{1,2},{2,3},{3,4},{4,5},{5,6},{6,7},{7,8},{8,9},{9,10},{10,1... | collective-permute-start | bytes 20 | tf_op jit(solution)/shard_map/while/body/eval_jaxpr/ppermute | solution.py:15
  240.3 14.0 %collective-permute-start.1 = (f32[1,1]{1,0:T(1,128)}, f32[1,1]{1,0:T(1,128)}, u32[]{:S(2)}, u32[]{:S(2)}) collective-permute-start(f32[1,1]{1,0:T(1,128)} %get-tuple-element.491), channel_id=1, source_target_pairs={{1,0},{2,1},{3,2},{4,3},{5,4},{6,5},{7,6},{8,7},{9,8},{10,9},{11,1... | collective-permute-start | bytes 20 | tf_op jit(solution)/shard_map/while/body/eval_jaxpr/while/body/eval_jaxpr/ppermute | solution.py:18
  241.6 12.8 %collective-permute-start.2 = (f32[1,1]{1,0:T(1,128)}, f32[1,1]{1,0:T(1,128)}, u32[]{:S(2)}, u32[]{:S(2)}) collective-permute-start(f32[1,1]{1,0:T(1,128)} %get-tuple-element.493), channel_id=1, source_target_pairs={{0,1},{1,2},{2,3},{3,4},{4,5},{5,6},{6,7},{7,8},{8,9},{9,10},{10,1... | collective-permute-start | bytes 20 | tf_op jit(solution)/shard_map/while/body/eval_jaxpr/while/body/eval_jaxpr/ppermute | solution.py:15
  247.7 11.9 %collective-permute-start.4 = (f32[1,1]{1,0:T(1,128)}, f32[1,1]{1,0:T(1,128)}, u32[]{:S(2)}, u32[]{:S(2)}) collective-permute-start(f32[1,1]{1,0:T(1,128)} %get-tuple-element.497), channel_id=1, source_target_pairs={{0,1},{1,2},{2,3},{3,4},{4,5},{5,6},{6,7},{7,8},{8,9},{9,10},{10,1... | collective-permute-start | bytes 20 | tf_op jit(solution)/shard_map/while/body/eval_jaxpr/ppermute | solution.py:15
  273.7 14.0 %collective-permute-start.1 = (f32[1,1]{1,0:T(1,128)}, f32[1,1]{1,0:T(1,128)}, u32[]{:S(2)}, u32[]{:S(2)}) collective-permute-start(f32[1,1]{1,0:T(1,128)} %get-tuple-element.491), channel_id=1, source_target_pairs={{1,0},{2,1},{3,2},{4,3},{5,4},{6,5},{7,6},{8,7},{9,8},{10,9},{11,1... | collective-permute-start | bytes 20 | tf_op jit(solution)/shard_map/while/body/eval_jaxpr/while/body/eval_jaxpr/ppermute | solution.py:18
  275.0 12.8 %collective-permute-start.2 = (f32[1,1]{1,0:T(1,128)}, f32[1,1]{1,0:T(1,128)}, u32[]{:S(2)}, u32[]{:S(2)}) collective-permute-start(f32[1,1]{1,0:T(1,128)} %get-tuple-element.493), channel_id=1, source_target_pairs={{0,1},{1,2},{2,3},{3,4},{4,5},{5,6},{6,7},{7,8},{8,9},{9,10},{10,1... | collective-permute-start | bytes 20 | tf_op jit(solution)/shard_map/while/body/eval_jaxpr/while/body/eval_jaxpr/ppermute | solution.py:15
  281.2 11.9 %collective-permute-start.4 = (f32[1,1]{1,0:T(1,128)}, f32[1,1]{1,0:T(1,128)}, u32[]{:S(2)}, u32[]{:S(2)}) collective-permute-start(f32[1,1]{1,0:T(1,128)} %get-tuple-element.497), channel_id=1, source_target_pairs={{0,1},{1,2},{2,3},{3,4},{4,5},{5,6},{6,7},{7,8},{8,9},{9,10},{10,1... | collective-permute-start | bytes 20 | tf_op jit(solution)/shard_map/while/body/eval_jaxpr/ppermute | solution.py:15
  307.1 14.0 %collective-permute-start.1 = (f32[1,1]{1,0:T(1,128)}, f32[1,1]{1,0:T(1,128)}, u32[]{:S(2)}, u32[]{:S(2)}) collective-permute-start(f32[1,1]{1,0:T(1,128)} %get-tuple-element.491), channel_id=1, source_target_pairs={{1,0},{2,1},{3,2},{4,3},{5,4},{6,5},{7,6},{8,7},{9,8},{10,9},{11,1... | collective-permute-start | bytes 20 | tf_op jit(solution)/shard_map/while/body/eval_jaxpr/while/body/eval_jaxpr/ppermute | solution.py:18
  308.4 12.8 %collective-permute-start.2 = (f32[1,1]{1,0:T(1,128)}, f32[1,1]{1,0:T(1,128)}, u32[]{:S(2)}, u32[]{:S(2)}) collective-permute-start(f32[1,1]{1,0:T(1,128)} %get-tuple-element.493), channel_id=1, source_target_pairs={{0,1},{1,2},{2,3},{3,4},{4,5},{5,6},{6,7},{7,8},{8,9},{9,10},{10,1... | collective-permute-start | bytes 20 | tf_op jit(solution)/shard_map/while/body/eval_jaxpr/while/body/eval_jaxpr/ppermute | solution.py:15
  314.6 11.9 %collective-permute-start.4 = (f32[1,1]{1,0:T(1,128)}, f32[1,1]{1,0:T(1,128)}, u32[]{:S(2)}, u32[]{:S(2)}) collective-permute-start(f32[1,1]{1,0:T(1,128)} %get-tuple-element.497), channel_id=1, source_target_pairs={{0,1},{1,2},{2,3},{3,4},{4,5},{5,6},{6,7},{7,8},{8,9},{9,10},{10,1... | collective-permute-start | bytes 20 | tf_op jit(solution)/shard_map/while/body/eval_jaxpr/ppermute | solution.py:15
  340.5 14.0 %collective-permute-start.1 = (f32[1,1]{1,0:T(1,128)}, f32[1,1]{1,0:T(1,128)}, u32[]{:S(2)}, u32[]{:S(2)}) collective-permute-start(f32[1,1]{1,0:T(1,128)} %get-tuple-element.491), channel_id=1, source_target_pairs={{1,0},{2,1},{3,2},{4,3},{5,4},{6,5},{7,6},{8,7},{9,8},{10,9},{11,1... | collective-permute-start | bytes 20 | tf_op jit(solution)/shard_map/while/body/eval_jaxpr/while/body/eval_jaxpr/ppermute | solution.py:18
  341.8 12.8 %collective-permute-start.2 = (f32[1,1]{1,0:T(1,128)}, f32[1,1]{1,0:T(1,128)}, u32[]{:S(2)}, u32[]{:S(2)}) collective-permute-start(f32[1,1]{1,0:T(1,128)} %get-tuple-element.493), channel_id=1, source_target_pairs={{0,1},{1,2},{2,3},{3,4},{4,5},{5,6},{6,7},{7,8},{8,9},{9,10},{10,1... | collective-permute-start | bytes 20 | tf_op jit(solution)/shard_map/while/body/eval_jaxpr/while/body/eval_jaxpr/ppermute | solution.py:15
  348.0 11.9 %collective-permute-start.4 = (f32[1,1]{1,0:T(1,128)}, f32[1,1]{1,0:T(1,128)}, u32[]{:S(2)}, u32[]{:S(2)}) collective-permute-start(f32[1,1]{1,0:T(1,128)} %get-tuple-element.497), channel_id=1, source_target_pairs={{0,1},{1,2},{2,3},{3,4},{4,5},{5,6},{6,7},{7,8},{8,9},{9,10},{10,1... | collective-permute-start | bytes 20 | tf_op jit(solution)/shard_map/while/body/eval_jaxpr/ppermute | solution.py:15
  373.9 14.0 %collective-permute-start.1 = (f32[1,1]{1,0:T(1,128)}, f32[1,1]{1,0:T(1,128)}, u32[]{:S(2)}, u32[]{:S(2)}) collective-permute-start(f32[1,1]{1,0:T(1,128)} %get-tuple-element.491), channel_id=1, source_target_pairs={{1,0},{2,1},{3,2},{4,3},{5,4},{6,5},{7,6},{8,7},{9,8},{10,9},{11,1... | collective-permute-start | bytes 20 | tf_op jit(solution)/shard_map/while/body/eval_jaxpr/while/body/eval_jaxpr/ppermute | solution.py:18
  375.2 12.8 %collective-permute-start.2 = (f32[1,1]{1,0:T(1,128)}, f32[1,1]{1,0:T(1,128)}, u32[]{:S(2)}, u32[]{:S(2)}) collective-permute-start(f32[1,1]{1,0:T(1,128)} %get-tuple-element.493), channel_id=1, source_target_pairs={{0,1},{1,2},{2,3},{3,4},{4,5},{5,6},{6,7},{7,8},{8,9},{9,10},{10,1... | collective-permute-start | bytes 20 | tf_op jit(solution)/shard_map/while/body/eval_jaxpr/while/body/eval_jaxpr/ppermute | solution.py:15
  381.4 11.9 %collective-permute-start.4 = (f32[1,1]{1,0:T(1,128)}, f32[1,1]{1,0:T(1,128)}, u32[]{:S(2)}, u32[]{:S(2)}) collective-permute-start(f32[1,1]{1,0:T(1,128)} %get-tuple-element.497), channel_id=1, source_target_pairs={{0,1},{1,2},{2,3},{3,4},{4,5},{5,6},{6,7},{7,8},{8,9},{9,10},{10,1... | collective-permute-start | bytes 20 | tf_op jit(solution)/shard_map/while/body/eval_jaxpr/ppermute | solution.py:15
  408.0 13.8 %collective-permute-start.1 = (f32[1,1]{1,0:T(1,128)}, f32[1,1]{1,0:T(1,128)}, u32[]{:S(2)}, u32[]{:S(2)}) collective-permute-start(f32[1,1]{1,0:T(1,128)} %get-tuple-element.491), channel_id=1, source_target_pairs={{1,0},{2,1},{3,2},{4,3},{5,4},{6,5},{7,6},{8,7},{9,8},{10,9},{11,1... | collective-permute-start | bytes 20 | tf_op jit(solution)/shard_map/while/body/eval_jaxpr/while/body/eval_jaxpr/ppermute | solution.py:18
  409.3 12.5 %collective-permute-start.2 = (f32[1,1]{1,0:T(1,128)}, f32[1,1]{1,0:T(1,128)}, u32[]{:S(2)}, u32[]{:S(2)}) collective-permute-start(f32[1,1]{1,0:T(1,128)} %get-tuple-element.493), channel_id=1, source_target_pairs={{0,1},{1,2},{2,3},{3,4},{4,5},{5,6},{6,7},{7,8},{8,9},{9,10},{10,1... | collective-permute-start | bytes 20 | tf_op jit(solution)/shard_map/while/body/eval_jaxpr/while/body/eval_jaxpr/ppermute | solution.py:15
  415.4 11.6 %collective-permute-start.4 = (f32[1,1]{1,0:T(1,128)}, f32[1,1]{1,0:T(1,128)}, u32[]{:S(2)}, u32[]{:S(2)}) collective-permute-start(f32[1,1]{1,0:T(1,128)} %get-tuple-element.497), channel_id=1, source_target_pairs={{0,1},{1,2},{2,3},{3,4},{4,5},{5,6},{6,7},{7,8},{8,9},{9,10},{10,1... | collective-permute-start | bytes 20 | tf_op jit(solution)/shard_map/while/body/eval_jaxpr/ppermute | solution.py:15
  442.6 13.8 %collective-permute-start.1 = (f32[1,1]{1,0:T(1,128)}, f32[1,1]{1,0:T(1,128)}, u32[]{:S(2)}, u32[]{:S(2)}) collective-permute-start(f32[1,1]{1,0:T(1,128)} %get-tuple-element.491), channel_id=1, source_target_pairs={{1,0},{2,1},{3,2},{4,3},{5,4},{6,5},{7,6},{8,7},{9,8},{10,9},{11,1... | collective-permute-start | bytes 20 | tf_op jit(solution)/shard_map/while/body/eval_jaxpr/while/body/eval_jaxpr/ppermute | solution.py:18
  443.9 12.5 %collective-permute-start.2 = (f32[1,1]{1,0:T(1,128)}, f32[1,1]{1,0:T(1,128)}, u32[]{:S(2)}, u32[]{:S(2)}) collective-permute-start(f32[1,1]{1,0:T(1,128)} %get-tuple-element.493), channel_id=1, source_target_pairs={{0,1},{1,2},{2,3},{3,4},{4,5},{5,6},{6,7},{7,8},{8,9},{9,10},{10,1... | collective-permute-start | bytes 20 | tf_op jit(solution)/shard_map/while/body/eval_jaxpr/while/body/eval_jaxpr/ppermute | solution.py:15
  450.0 11.6 %collective-permute-start.4 = (f32[1,1]{1,0:T(1,128)}, f32[1,1]{1,0:T(1,128)}, u32[]{:S(2)}, u32[]{:S(2)}) collective-permute-start(f32[1,1]{1,0:T(1,128)} %get-tuple-element.497), channel_id=1, source_target_pairs={{0,1},{1,2},{2,3},{3,4},{4,5},{5,6},{6,7},{7,8},{8,9},{9,10},{10,1... | collective-permute-start | bytes 20 | tf_op jit(solution)/shard_map/while/body/eval_jaxpr/ppermute | solution.py:15
  477.2 13.8 %collective-permute-start.1 = (f32[1,1]{1,0:T(1,128)}, f32[1,1]{1,0:T(1,128)}, u32[]{:S(2)}, u32[]{:S(2)}) collective-permute-start(f32[1,1]{1,0:T(1,128)} %get-tuple-element.491), channel_id=1, source_target_pairs={{1,0},{2,1},{3,2},{4,3},{5,4},{6,5},{7,6},{8,7},{9,8},{10,9},{11,1... | collective-permute-start | bytes 20 | tf_op jit(solution)/shard_map/while/body/eval_jaxpr/while/body/eval_jaxpr/ppermute | solution.py:18
  478.5 12.5 %collective-permute-start.2 = (f32[1,1]{1,0:T(1,128)}, f32[1,1]{1,0:T(1,128)}, u32[]{:S(2)}, u32[]{:S(2)}) collective-permute-start(f32[1,1]{1,0:T(1,128)} %get-tuple-element.493), channel_id=1, source_target_pairs={{0,1},{1,2},{2,3},{3,4},{4,5},{5,6},{6,7},{7,8},{8,9},{9,10},{10,1... | collective-permute-start | bytes 20 | tf_op jit(solution)/shard_map/while/body/eval_jaxpr/while/body/eval_jaxpr/ppermute | solution.py:15
  484.7 11.6 %collective-permute-start.4 = (f32[1,1]{1,0:T(1,128)}, f32[1,1]{1,0:T(1,128)}, u32[]{:S(2)}, u32[]{:S(2)}) collective-permute-start(f32[1,1]{1,0:T(1,128)} %get-tuple-element.497), channel_id=1, source_target_pairs={{0,1},{1,2},{2,3},{3,4},{4,5},{5,6},{6,7},{7,8},{8,9},{9,10},{10,1... | collective-permute-start | bytes 20 | tf_op jit(solution)/shard_map/while/body/eval_jaxpr/ppermute | solution.py:15
  511.8 13.8 %collective-permute-start.1 = (f32[1,1]{1,0:T(1,128)}, f32[1,1]{1,0:T(1,128)}, u32[]{:S(2)}, u32[]{:S(2)}) collective-permute-start(f32[1,1]{1,0:T(1,128)} %get-tuple-element.491), channel_id=1, source_target_pairs={{1,0},{2,1},{3,2},{4,3},{5,4},{6,5},{7,6},{8,7},{9,8},{10,9},{11,1... | collective-permute-start | bytes 20 | tf_op jit(solution)/shard_map/while/body/eval_jaxpr/while/body/eval_jaxpr/ppermute | solution.py:18
  513.1 12.5 %collective-permute-start.2 = (f32[1,1]{1,0:T(1,128)}, f32[1,1]{1,0:T(1,128)}, u32[]{:S(2)}, u32[]{:S(2)}) collective-permute-start(f32[1,1]{1,0:T(1,128)} %get-tuple-element.493), channel_id=1, source_target_pairs={{0,1},{1,2},{2,3},{3,4},{4,5},{5,6},{6,7},{7,8},{8,9},{9,10},{10,1... | collective-permute-start | bytes 20 | tf_op jit(solution)/shard_map/while/body/eval_jaxpr/while/body/eval_jaxpr/ppermute | solution.py:15
  519.3 11.6 %collective-permute-start.4 = (f32[1,1]{1,0:T(1,128)}, f32[1,1]{1,0:T(1,128)}, u32[]{:S(2)}, u32[]{:S(2)}) collective-permute-start(f32[1,1]{1,0:T(1,128)} %get-tuple-element.497), channel_id=1, source_target_pairs={{0,1},{1,2},{2,3},{3,4},{4,5},{5,6},{6,7},{7,8},{8,9},{9,10},{10,1... | collective-permute-start | bytes 20 | tf_op jit(solution)/shard_map/while/body/eval_jaxpr/ppermute | solution.py:15
  546.5 13.8 %collective-permute-start.1 = (f32[1,1]{1,0:T(1,128)}, f32[1,1]{1,0:T(1,128)}, u32[]{:S(2)}, u32[]{:S(2)}) collective-permute-start(f32[1,1]{1,0:T(1,128)} %get-tuple-element.491), channel_id=1, source_target_pairs={{1,0},{2,1},{3,2},{4,3},{5,4},{6,5},{7,6},{8,7},{9,8},{10,9},{11,1... | collective-permute-start | bytes 20 | tf_op jit(solution)/shard_map/while/body/eval_jaxpr/while/body/eval_jaxpr/ppermute | solution.py:18
  547.8 12.5 %collective-permute-start.2 = (f32[1,1]{1,0:T(1,128)}, f32[1,1]{1,0:T(1,128)}, u32[]{:S(2)}, u32[]{:S(2)}) collective-permute-start(f32[1,1]{1,0:T(1,128)} %get-tuple-element.493), channel_id=1, source_target_pairs={{0,1},{1,2},{2,3},{3,4},{4,5},{5,6},{6,7},{7,8},{8,9},{9,10},{10,1... | collective-permute-start | bytes 20 | tf_op jit(solution)/shard_map/while/body/eval_jaxpr/while/body/eval_jaxpr/ppermute | solution.py:15
  553.9 11.6 %collective-permute-start.4 = (f32[1,1]{1,0:T(1,128)}, f32[1,1]{1,0:T(1,128)}, u32[]{:S(2)}, u32[]{:S(2)}) collective-permute-start(f32[1,1]{1,0:T(1,128)} %get-tuple-element.497), channel_id=1, source_target_pairs={{0,1},{1,2},{2,3},{3,4},{4,5},{5,6},{6,7},{7,8},{8,9},{9,10},{10,1... | collective-permute-start | bytes 20 | tf_op jit(solution)/shard_map/while/body/eval_jaxpr/ppermute | solution.py:15
  (57 other events, 460.3 us)
where the time goes:
time: 693 us; the launch traced here: 681 us
  starting transfers between devices  329 us (47%)
  other arithmetic  138 us (20%)
  blocking collectives  108 us (16%)
  local copies, waits for them, and re-layouts  101 us (15%)
    ppermute x34, starting transfers between devices, extended(): lax.ppermute(lax.slice_in_dim(block, block.shape[dim] - width, None, axis...  172 us
    ppermute x34, starting transfers between devices, passed_along(): return lax.ppermute(array, axis, pairs)  114 us
    mul x17, other arithmetic, backward_block(): outgoing = emission_block[0].astype(jnp.float32) * first_field  64.5 us
    select_n x17, other arithmetic, section_step(): jnp.where(forward_valid, new_alphas, take_rows(alphas_now, forward_start,...  61.3 us
    psum x1, blocking collectives, body(): totals = lax.psum((members[0], members[1]), 'freq')  59.7 us
    psum x1, blocking collectives, body(): evidence = lax.psum(growth, 'tm') / (groups * steps_here)  48.4 us
    ppermute x34, starting transfers between devices, extended(): lax.ppermute(lax.slice_in_dim(block, 0, width, axis=dim), axis, backward)  43.5 us
    dynamic_update_slice x17, local copies, waits for them, and re-layouts, section_step(): lax.dynamic_update_slice_in_dim(betas_now, jnp.where(backward_valid, new_...  28 us
  transfers between devices with their start and end apart: 102, of which 0 were waited for; matrix products, arithmetic and copies ran while one was open for 20% of the time, Pallas kernels for 0%

commit v1 on v0

v1 whole, which is shorter than its diff:
```python
import functools

import jax
import jax.numpy as jnp
from jax import lax
from jax.experimental import pallas as pl
from jax.experimental.pallas import tpu as pltpu
from jax.sharding import PartitionSpec as P

MESH = pl.DeviceIdType.MESH
Z_CHIPS = 8
LANES = 128
TAIL = 8


def ring_order(chips):
    steps = [chips // 2]
    for d in range(chips // 2 - 1, 0, -1):
        steps += [-d, d]
    return [(d, c) for d in steps for c in (0, 1)] + [(0, 1)]


def kernel(groups, freqs, zs, bins, x_hbm, w_hbm, ids_hbm, post_ref, level_ref,
           x_half, x_full, w_ref, ids_ref, stage, recv, halo, edge, beside, work,
           part, part_in, z_part, z_in, x_part, x_in, home, relay, relay_back,
           load_sem, send_sem, recv_sem, edge_send, edge_recv, halo_send, halo_recv, back_send, back_recv,
           part_send, part_recv, z_send, z_recv, x_send, x_recv, own_sem,
           relay_recv, pass_send):
    xs = freqs // zs
    chips = groups // 2
    tm = lax.axis_index("tm")
    fq = lax.axis_index("freq")
    yi = tm // 2
    core = lax.rem(tm, 2)
    xi = fq // zs
    zi = lax.rem(fq, zs)
    next_fq = lax.rem(fq + 1, freqs)
    prev_fq = lax.rem(fq + freqs - 1, freqs)
    all_rows = x_hbm.shape[0]
    rows = all_rows // groups
    last = groups - 1
    order = ring_order(chips)

    def member(k):
        return lax.rem(yi + k[0] + chips, chips) * 2 + lax.rem(core + k[1], 2)

    loads = [pltpu.make_async_copy(src, dst, load_sem.at[i])
             for i, (src, dst) in enumerate(((x_hbm, x_half), (w_hbm, w_ref), (ids_hbm, ids_ref)))]
    for copy in loads:
        copy.start()

    barrier = pltpu.get_barrier_semaphore()

    def greet(t, f):
        pl.semaphore_signal(barrier, inc=1, device_id=(t, f), device_id_type=MESH)

    def across_x(k):
        place = lax.rem(xi * 2 + core + k, 2 * xs)
        return place, (yi * 2 + lax.rem(place, 2), place // 2 * zs + zi)

    peers = [(min(abs(k[0]), chips - abs(k[0])), member(k), fq) for k in order]
    peers += [(min(k, zs - k), tm, xi * zs + lax.rem(zi + k, zs)) for k in range(1, zs)]
    peers += [(min(k // 2, xs - k // 2), *across_x(k)[1]) for k in range(1, 2 * xs)]
    for _, t, f in sorted(peers, key=lambda peer: -peer[0]):
        greet(t, f)
    has_next = fq < freqs - 1
    has_prev = fq > 0
    next_turns = has_next & (zi == zs - 1)
    prev_turns = has_prev & (zi == 0)
    low_halo = (yi == 0) & has_prev
    high_halo = (yi == chips - 1) & has_next

    @pl.when(next_turns)
    def _():
        greet(tm, next_fq)

    @pl.when(prev_turns)
    def _():
        greet(tm, prev_fq)

    loads[0].wait()
    for r in range(0, all_rows, 16):
        x_full[r:r + 16, :] = x_half[r:r + 16, :].astype(jnp.float32)
    low_lanes = lax.broadcasted_iota(jnp.int32, (1, LANES), 1) < LANES // 2
    nothing = jnp.zeros((1, LANES), jnp.float32)
    for o in range(chips):
        for p in range(2):
            first = 2 * o * rows + p
            for r in range(0, rows, 8):
                stage[2 * o + p, r:r + 8, :] = x_full[pl.ds(first + 2 * r, 8, stride=2), :]
            after = first + 2 * rows
            high = x_full[after:after + 1, :] if o < chips - 1 else nothing
            low = x_full[first - 2:first - 1, :] if o > 0 else nothing
            stage[2 * o + p, rows:rows + 1, :] = jnp.where(low_lanes, high, low)
    for p in range(2):
        edge[0, p] = x_full[all_rows - 2 + p:all_rows - 1 + p, :]
        edge[1, p] = x_full[p:p + 1, :]

    expected = (groups - 1) + (zs - 1) + (2 * xs - 1)
    pl.semaphore_wait(barrier, expected + next_turns.astype(jnp.int32) + prev_turns.astype(jnp.int32))

    def remote(src, dst, s_sem, r_sem, to):
        return pltpu.make_async_remote_copy(
            src_ref=src, dst_ref=dst, send_sem=s_sem, recv_sem=r_sem, device_id=to, device_id_type=MESH)

    def all_of(ref, count, sem):
        block = ref.at[pl.ds(0, count)]
        pltpu.make_async_copy(block, block, sem).wait()

    def out_copy(k):
        to = member(k)
        return remote(stage.at[to], recv.at[tm], send_sem.at[0], recv_sem.at[0], (to, fq))

    def edge_copy(side, to):
        return remote(edge.at[side], beside.at[side], edge_send.at[side], edge_recv.at[side], (tm, to))

    def halo_copy(side, p):
        owner = p if side == 0 else last - 1 + p
        to = jnp.where(tm == owner, owner + 1 - 2 * p, owner)
        return tm == owner, remote(
            beside.at[side, p], halo.at[tm], halo_send.at[side, p], halo_recv.at[0], (to, fq))

    def halo_pass(side):
        edge_copy(side, fq).wait_recv()
        for p in range(2):
            here, copy = halo_copy(side, p)

            @pl.when(here)
            def _():
                pltpu.make_async_copy(beside.at[side, p], halo.at[tm], halo_recv.at[0]).start()

            @pl.when(jnp.logical_not(here))
            def _():
                copy.start()

    def halo_sent(side):
        for p in range(2):
            here, copy = halo_copy(side, p)

            @pl.when(jnp.logical_not(here))
            def _():
                copy.wait_send()

    @pl.when(has_next)
    def _():
        edge_copy(0, next_fq).start()

    @pl.when(has_prev)
    def _():
        edge_copy(1, prev_fq).start()

    far = chips // 2
    near = far // 2
    direct = [k for k in order if k[0] != far]

    def relay_copy(src, dst, phase, c):
        way = near if c == 0 else -near
        return remote(src.at[member((far, lax.rem(core + c, 2)))], dst.at[c],
                      (send_sem, back_send)[phase].at[0], relay_recv.at[phase, c], (member((way, 0)), fq))

    def pass_copy(src, dst, r_sem, phase, c):
        way = near if c == 0 else -near
        origin = member((-way, 0))
        return remote(src.at[c], dst.at[origin], pass_send.at[phase], r_sem.at[0],
                      (member((way, lax.rem(core + c, 2))), fq))

    for c in (0, 1):
        relay_copy(stage, relay, 0, c).start()
    for k in direct:
        out_copy(k).start()

    @pl.when(has_prev)
    def _():
        halo_pass(0)

    @pl.when(has_next)
    def _():
        halo_pass(1)

    own = pltpu.make_async_copy(stage.at[tm], recv.at[tm], own_sem.at[0])
    own.start()

    for c in (0, 1):
        relay_copy(stage, relay, 0, c).wait_recv()
        pass_copy(relay, recv, recv_sem, 0, c).start()

    loads[1].wait()
    loads[2].wait()
    slot = lax.broadcasted_iota(jnp.int32, w_ref.shape, 1)
    weights = jnp.sum(jnp.where(slot == ids_ref[core], w_ref[...], 0.0), axis=1, keepdims=True)
    weights = weights / jnp.sum(weights, axis=0, keepdims=True)
    field = (rows + TAIL, LANES)
    staying, rising, falling = (jnp.broadcast_to(weights[i:i + 1, :], field) for i in range(3))
    lane = lax.broadcasted_iota(jnp.int32, field, 1)
    row_index = lax.broadcasted_iota(jnp.int32, field, 0)

    from_other = (high_halo & low_lanes) | (low_halo & jnp.logical_not(low_lanes))

    def emission_of(t):
        tail = jnp.where(from_other, halo[t], recv[t, rows:rows + 1, :])
        return jnp.concatenate([recv[t, 0:rows, :], jnp.broadcast_to(tail, (TAIL, LANES))], axis=0)

    def below(v):
        turned = pltpu.roll(v, 1, 1)
        return jnp.where(lane == 0, pltpu.roll(turned, 1, 0), turned)

    def above(v):
        turned = pltpu.roll(v, LANES - 1, 1)
        return jnp.where(lane == LANES - 1, pltpu.roll(turned, field[0] - 1, 0), turned)

    own.wait()
    all_of(recv, groups - 1, recv_sem.at[0])

    @pl.when(low_halo | high_halo)
    def _():
        all_of(halo, groups, halo_recv.at[0])

    world_low = (yi == 0) & (fq == 0)
    world_high = (yi == chips - 1) & (fq == freqs - 1)
    outside = ((row_index == rows) & world_high) | ((row_index > rows) & world_low)
    b = jnp.ones(field, jnp.float32)
    u = jnp.where(outside, 0.0, b)

    def forward(t, u):
        return emission_of(t) * (staying * u + rising * below(u) + falling * above(u))

    def backward(s, b):
        g = emission_of(s + 1) * b
        return staying * g + rising * above(g) + falling * below(g)

    half = groups // 2
    for step in range(half):
        u = forward(step, u)
        work[step] = u[:rows]
        if step > 0:
            b = backward(last - step, b)
        work[last - step] = b[:rows]
    b = backward(half - 1, b)
    middle = u[:rows] * b[:rows]
    work[half - 1] = middle
    part[...] = jnp.sum(middle, axis=0, keepdims=True)

    def spread(src, dst, to_of, mine, count, s_sem, r_sem):
        for k in range(1, count):
            remote(src, dst.at[mine], s_sem.at[0], r_sem.at[0], to_of(k)).start()

    def gather(src, dst, to_of, mine, count, s_sem, r_sem):
        all_of(dst, count - 1, r_sem.at[0])
        value = src[...]
        for k in range(1, count):
            value = value + dst[lax.rem(mine + k, count)]
        return value

    y_ring = (lambda k: (lax.rem(yi + k, chips) * 2 + core, fq), yi, chips, part_send, part_recv)
    z_ring = (lambda k: (tm, xi * zs + lax.rem(zi + k, zs)), zi, zs, z_send, z_recv)
    x_ring = (lambda k: across_x(k)[1], xi * 2 + core, 2 * xs, x_send, x_recv)
    spread(part, part_in, *y_ring)

    for step in range(half, groups):
        u = forward(step, u)
        work[step] = u[:rows] * work[step]
        if step > half:
            b = backward(last - step, b)
            work[last - step] = work[last - step] * b[:rows]

    def back_copy(k):
        to = member(k)
        return remote(work.at[to], home.at[tm], back_send.at[0], back_recv.at[0], (to, fq))

    own_back = pltpu.make_async_copy(work.at[tm], home.at[tm], own_sem.at[1])
    own_back.start()
    for c in (0, 1):
        relay_copy(work, relay_back, 1, c).start()
    for k in direct:
        back_copy(k).start()

    z_part[...] = gather(part, part_in, *y_ring)
    spread(z_part, z_in, *z_ring)
    for c in (0, 1):
        relay_copy(work, relay_back, 1, c).wait_recv()
        pass_copy(relay_back, home, back_recv, 1, c).start()
    all_of(stage, groups - 1, send_sem.at[0])
    all_of(relay, 2, pass_send.at[0])

    x_part[...] = gather(z_part, z_in, *z_ring)
    spread(x_part, x_in, *x_ring)

    @pl.when(has_next)
    def _():
        edge_copy(0, next_fq).wait_send()
        halo_sent(1)

    @pl.when(has_prev)
    def _():
        edge_copy(1, prev_fq).wait_send()
        halo_sent(0)

    all_of(part_in, chips - 1, part_send.at[0])
    all_of(z_in, zs - 1, z_send.at[0])
    all_of(x_in, 2 * xs - 1, x_recv.at[0])
    same = x_part[...]
    other = jnp.zeros_like(same)
    for k in range(1, 2 * xs):
        place, _ = across_x(k)
        if k % 2 == 0:
            same = same + x_in[place]
        else:
            other = other + x_in[place]
    totals = []
    for p in range(2):
        whole = jnp.sum(jnp.where(core == p, same, other), axis=1, keepdims=True)
        totals.append(whole)
        level_ref[p] = (jnp.log(whole * (1.0 / bins)) * (1.0 / groups))[0, 0]

    def settle(source):
        parity = lax.rem(source, 2)
        scale = bins / jnp.where(parity == 0, totals[0], totals[1])
        first_row = source // 2 * (2 * rows) + parity
        for r in range(0, rows, 8):
            post_ref[pl.ds(first_row + 2 * r, 8, stride=2), :] = home[source, r:r + 8, :] * scale

    own_back.wait()
    all_of(home, groups - 1, back_recv.at[0])
    settle(tm)
    for k in order:
        settle(member(k))
    all_of(x_in, 2 * xs - 1, x_send.at[0])
    all_of(work, groups - 1, back_send.at[0])
    all_of(relay_back, 2, pass_send.at[1])


def body(bins, groups, freqs, zs, emission, step_weights, template_ids):
    templates = emission.shape[1]
    here = emission.shape[2]
    total_rows = here // LANES
    all_rows = templates * total_rows
    rows = all_rows // groups
    xs = freqs // zs
    f32 = jnp.float32
    dma = pltpu.SemaphoreType.DMA
    lines = emission.reshape(templates, total_rows, LANES).transpose(1, 0, 2).reshape(all_rows, LANES)
    hbm = pl.BlockSpec(memory_space=pltpu.HBM)
    vmem = pl.BlockSpec(memory_space=pltpu.VMEM)
    post, level = pl.pallas_call(
        functools.partial(kernel, groups, freqs, zs, bins),
        out_shape=(
            jax.ShapeDtypeStruct((all_rows, LANES), f32),
            jax.ShapeDtypeStruct((templates,), f32),
        ),
        in_specs=[hbm, hbm, hbm],
        out_specs=(vmem, pl.BlockSpec(memory_space=pltpu.SMEM)),
        scratch_shapes=[
            pltpu.VMEM((all_rows, LANES), emission.dtype),
            pltpu.VMEM((all_rows, LANES), f32),
            pltpu.VMEM((step_weights.shape[1], step_weights.shape[0]), f32),
            pltpu.SMEM(template_ids.shape, jnp.int32),
            pltpu.VMEM((groups, rows + 1, LANES), f32),
            pltpu.VMEM((groups, rows + 1, LANES), f32),
            pltpu.VMEM((groups, 1, LANES), f32),
            pltpu.VMEM((2, 2, 1, LANES), f32),
            pltpu.VMEM((2, 2, 1, LANES), f32),
            pltpu.VMEM((groups, rows, LANES), f32),
            pltpu.VMEM((1, LANES), f32),
            pltpu.VMEM((groups // 2, 1, LANES), f32),
            pltpu.VMEM((1, LANES), f32),
            pltpu.VMEM((zs, 1, LANES), f32),
            pltpu.VMEM((1, LANES), f32),
            pltpu.VMEM((2 * xs, 1, LANES), f32),
            pltpu.VMEM((groups, rows, LANES), f32),
            pltpu.VMEM((2, rows + 1, LANES), f32),
            pltpu.VMEM((2, rows, LANES), f32),
            dma((3,)), dma((1,)), dma((1,)), dma((2,)), dma((2,)), dma((2, 2)), dma((1,)), dma((1,)), dma((1,)),
            dma((1,)), dma((1,)), dma((1,)), dma((1,)), dma((1,)), dma((1,)), dma((2,)),
            dma((2, 2)), dma((2,)),
        ],
        compiler_params=pltpu.CompilerParams(
            collective_id=0, has_side_effects=True, vmem_limit_bytes=32 * 1024 * 1024
        ),
    )(*(pltpu.with_memory_space_constraint(v, pltpu.HBM) for v in (lines, step_weights.T, template_ids)))
    posterior = post.reshape(total_rows, templates, LANES).transpose(1, 0, 2).reshape(1, templates, here)
    return posterior, level


def solution(mesh):
    groups, freqs = mesh.shape["tm"], mesh.shape["freq"]
    zs = min(Z_CHIPS, freqs // 2)

    def whole(emission, step_weights, template_ids):
        return jax.shard_map(
            functools.partial(body, emission.shape[2], groups, freqs, zs),
            mesh=mesh,
            in_specs=(P("tm", None, "freq"), P(), P()),
            out_specs=(P("tm", None, "freq"), P()),
            check_vma=False,
        )(emission, step_weights, template_ids)

    return whole
```

time: 693 us -> 39.6 us (0.06); the launches traced: 681 us -> 39.5 us
  starting transfers between devices: 329 us -> 0 us
  other arithmetic: 138 us -> 0 us
  blocking collectives: 108 us -> 0 us
  local copies, waits for them, and re-layouts: 101 us -> 1.22 us
  Pallas kernels: 0 us -> 37.7 us
    ppermute x102 -> x0, starting transfers between devices: 329 us -> none  [the longest x34 172 us: extended(): lax.ppermute(lax.slice_in_dim(block, block.shape[dim] - width, None, axis...]
    psum x2 -> x0, blocking collectives: 108 us -> none  [the longest x1 59.7 us: body(): totals = lax.psum((members[0], members[1]), 'freq')]
    select_n x69 -> x0, other arithmetic: 68 us -> none  [the longest x17 61.3 us: section_step(): jnp.where(forward_valid, new_alphas, take_rows(alphas_now, forward_start,...]
    mul x17 -> x0, other arithmetic: 64.5 us -> none  [backward_block(): outgoing = emission_block[0].astype(jnp.float32) * first_field]
    dynamic_update_slice x34 -> x0, local copies, waits for them, and re-layouts: 56 us -> none  [the longest x17 28 us: section_step(): lax.dynamic_update_slice_in_dim(betas_now, jnp.where(backward_valid, new_...]
    pallas_call x0 -> x1, Pallas kernels: none -> 37.7 us  [body(): pl.pallas_call(functools.partial(kernel, groups, freqs, zs, bins), out_sh...]
    dynamic_slice x34 -> x0, local copies, waits for them, and re-layouts: 22.1 us -> none  [take_rows(): return lax.dynamic_slice_in_dim(array, start, batch_rows, axis)]
    slice x35 -> x0, local copies, waits for them, and re-layouts: 21.2 us -> none  [the longest x17 11.2 us: extended(): lax.slice_in_dim(block, 0, width, axis=dim)]
  transfers between devices with their start and end apart: 102 -> 0, of which waited for: 0 -> 0; matrix products, arithmetic and copies ran while one was open for 20% -> 0% of each run, Pallas kernels for 0% -> 0%
where the time goes in v1:
time: 39.6 us; the launch traced here: 39.5 us
  Pallas kernels  37.7 us (95%)
  local copies, waits for them, and re-layouts  1.22 us (3%)
  between operations  0.64 us (2%)
    pallas_call x1, Pallas kernels, body(): pl.pallas_call(functools.partial(kernel, groups, freqs, zs, bins), out_sh...  37.7 us
    unnamed x2, local copies, waits for them, and re-layouts  1.22 us

profile of v1, /device:TPU:1, one launch (start us, length us, event | category | flops | bytes accessed | tf_op | source)
XLA Modules:
  0.0 39.5 jit_solution(15795351781261856107)
XLA Ops:
  0.6 37.7 %shard_map.50 = (f32[512,128]{1,0:T(8,128)S(1)}, f32[2]{0:T(128)S(1)}) custom-call(bf16[512,128]{1,0:T(8,128)(2,1)} %bitcast.12, f32[3,64]{1,0:T(4,128)} %bitcast.13, s32[2]{0:T(128)} %ids_hbm.1), custom_call_target="tpu_custom_call" | custom-call | tf_op jit(solution)/shard_map/pallas_call | solution.py:344
  38.3 0.7 %copy.9 = f32[1,2,32768]{2,1,0:T(2,128)} copy(f32[1,2,32768]{2,1,0:T(2,128)S(1)} %bitcast.11) | data formatting | bytes 524288
  39.0 0.5 %copy.10 = f32[2]{0:T(128)} copy(f32[2]{0:T(128)S(1)} %get-tuple-element.9) | data formatting | bytes 16

commit v2 on v1

--- a/solution.py
+++ b/solution.py
@@ -20,9 +20,9 @@
     return [(d, c) for d in steps for c in (0, 1)] + [(0, 1)]
 
 
-def kernel(groups, freqs, zs, bins, x_hbm, w_hbm, ids_hbm, post_ref, level_ref,
+def kernel(groups, freqs, zs, bins, x_hbm, w_hbm, ids_hbm, home, total_ref,
            x_half, x_full, w_ref, ids_ref, stage, recv, halo, edge, beside, work,
-           part, part_in, z_part, z_in, x_part, x_in, home, relay, relay_back,
+           part, part_in, z_part, z_in, x_part, x_in, relay, relay_back,
            load_sem, send_sem, recv_sem, edge_send, edge_recv, halo_send, halo_recv, back_send, back_recv,
            part_send, part_recv, z_send, z_recv, x_send, x_recv, own_sem,
            relay_recv, pass_send):
@@ -271,11 +271,13 @@
     own_back.start()
     for c in (0, 1):
         relay_copy(work, relay_back, 1, c).start()
-    for k in direct:
+    for k in direct[:len(direct) // 2]:
         back_copy(k).start()
 
     z_part[...] = gather(part, part_in, *y_ring)
     spread(z_part, z_in, *z_ring)
+    for k in direct[len(direct) // 2:]:
+        back_copy(k).start()
     for c in (0, 1):
         relay_copy(work, relay_back, 1, c).wait_recv()
         pass_copy(relay_back, home, back_recv, 1, c).start()
@@ -306,27 +308,37 @@
             same = same + x_in[place]
         else:
             other = other + x_in[place]
-    totals = []
     for p in range(2):
         whole = jnp.sum(jnp.where(core == p, same, other), axis=1, keepdims=True)
-        totals.append(whole)
-        level_ref[p] = (jnp.log(whole * (1.0 / bins)) * (1.0 / groups))[0, 0]
-
-    def settle(source):
-        parity = lax.rem(source, 2)
-        scale = bins / jnp.where(parity == 0, totals[0], totals[1])
-        first_row = source // 2 * (2 * rows) + parity
-        for r in range(0, rows, 8):
-            post_ref[pl.ds(first_row + 2 * r, 8, stride=2), :] = home[source, r:r + 8, :] * scale
+        total_ref[p:p + 1, :] = jnp.broadcast_to(whole, (1, LANES))
 
     own_back.wait()
     all_of(home, groups - 1, back_recv.at[0])
-    settle(tm)
-    for k in order:
-        settle(member(k))
     all_of(x_in, 2 * xs - 1, x_send.at[0])
     all_of(work, groups - 1, back_send.at[0])
     all_of(relay_back, 2, pass_send.at[1])
+
+
+def finish(bins, home, total_ref, out_hbm, level_hbm, out, level, sems):
+    groups, rows = home.shape[0], home.shape[1]
+    totals = [total_ref[p:p + 1, :] for p in range(2)]
+    scales = [bins / total for total in totals]
+    blocks = groups // 2
+    copies = []
+    for o in range(blocks):
+        first = o * 2 * rows
+        for p in range(2):
+            for r in range(0, rows, 8):
+                out[pl.ds(first + p + 2 * r, 8, stride=2), :] = home[2 * o + p, r:r + 8, :] * scales[p]
+        block = pl.ds(first, 2 * rows)
+        copies.append(pltpu.make_async_copy(out.at[block, :], out_hbm.at[block, :], sems.at[o]))
+        copies[-1].start()
+    for p in range(2):
+        level[p] = (jnp.log(totals[p] * (1.0 / bins)) * (1.0 / groups))[0, 0]
+    copies.append(pltpu.make_async_copy(level, level_hbm, sems.at[blocks]))
+    copies[-1].start()
+    for copy in copies:
+        copy.wait()
 
 
 def body(bins, groups, freqs, zs, emission, step_weights, template_ids):
@@ -341,14 +353,14 @@
     lines = emission.reshape(templates, total_rows, LANES).transpose(1, 0, 2).reshape(all_rows, LANES)
     hbm = pl.BlockSpec(memory_space=pltpu.HBM)
     vmem = pl.BlockSpec(memory_space=pltpu.VMEM)
-    post, level = pl.pallas_call(
+    home, total = pl.pallas_call(
         functools.partial(kernel, groups, freqs, zs, bins),
         out_shape=(
-            jax.ShapeDtypeStruct((all_rows, LANES), f32),
-            jax.ShapeDtypeStruct((templates,), f32),
+            jax.ShapeDtypeStruct((groups, rows, LANES), f32),
+            jax.ShapeDtypeStruct((templates, LANES), f32),
         ),
         in_specs=[hbm, hbm, hbm],
-        out_specs=(vmem, pl.BlockSpec(memory_space=pltpu.SMEM)),
+        out_specs=(vmem, vmem),
         scratch_shapes=[
             pltpu.VMEM((all_rows, LANES), emission.dtype),
             pltpu.VMEM((all_rows, LANES), f32),
@@ -366,7 +378,6 @@
             pltpu.VMEM((zs, 1, LANES), f32),
             pltpu.VMEM((1, LANES), f32),
             pltpu.VMEM((2 * xs, 1, LANES), f32),
-            pltpu.VMEM((groups, rows, LANES), f32),
             pltpu.VMEM((2, rows + 1, LANES), f32),
             pltpu.VMEM((2, rows, LANES), f32),
             dma((3,)), dma((1,)), dma((1,)), dma((2,)), dma((2,)), dma((2, 2)), dma((1,)), dma((1,)), dma((1,)),
@@ -377,6 +388,18 @@
             collective_id=0, has_side_effects=True, vmem_limit_bytes=32 * 1024 * 1024
         ),
     )(*(pltpu.with_memory_space_constraint(v, pltpu.HBM) for v in (lines, step_weights.T, template_ids)))
+    anywhere = pl.BlockSpec(memory_space=pl.ANY)
+    post, level = pl.pallas_call(
+        functools.partial(finish, bins),
+        out_shape=(
+            jax.ShapeDtypeStruct((all_rows, LANES), f32),
+            jax.ShapeDtypeStruct((templates,), f32),
+        ),
+        in_specs=[vmem, vmem],
+        out_specs=(anywhere, anywhere),
+        scratch_shapes=[pltpu.VMEM((all_rows, LANES), f32), pltpu.SMEM((templates,), f32), dma((groups // 2 + 1,))],
+        compiler_params=pltpu.CompilerParams(vmem_limit_bytes=4 * 1024 * 1024),
+    )(home, total)
     posterior = post.reshape(total_rows, templates, LANES).transpose(1, 0, 2).reshape(1, templates, here)
     return posterior, level
 

time: 39.6 us -> 37.9 us (0.957)
  local copies, waits for them, and re-layouts: 1.22 us -> 0 us
  Pallas kernels: 37.7 us -> 37.1 us
    pallas_call x1, Pallas kernels: 37.7 us -> 36.3 us  [body(): pl.pallas_call(functools.partial(kernel, groups, freqs, zs, bins), out_sh...]
    unnamed x2 -> x0, local copies, waits for them, and re-layouts: 1.22 us -> none
    pallas_call x0 -> x1, Pallas kernels: none -> 0.79 us  [body(): pl.pallas_call(functools.partial(finish, bins), out_shape=(jax.ShapeDtype...]
where the time goes in v2:
time: 37.9 us; the launch traced here: 37.8 us
  Pallas kernels  37.1 us (98%)
  between operations  0.64 us (2%)
    pallas_call x1, Pallas kernels, body(): pl.pallas_call(functools.partial(kernel, groups, freqs, zs, bins), out_sh...  36.3 us
    pallas_call x1, Pallas kernels, body(): pl.pallas_call(functools.partial(finish, bins), out_shape=(jax.ShapeDtype...  0.79 us

profile of v2, /device:TPU:1, one launch (start us, length us, event | category | flops | bytes accessed | tf_op | source)
XLA Modules:
  0.0 37.8 jit_solution(16867566269272387006)
XLA Ops:
  0.6 36.3 %shard_map.50 = (f32[16,32,128]{2,1,0:T(8,128)S(1)}, f32[2,128]{1,0:T(2,128)S(1)}) custom-call(bf16[512,128]{1,0:T(8,128)(2,1)} %bitcast.11, f32[3,64]{1,0:T(4,128)} %bitcast.12, s32[2]{0:T(128)} %ids_hbm.1), custom_call_target="tpu_custom_call" | custom-call | tf_op jit(solution)/shard_map/pallas_call | solution.py:356
  37.0 0.8 %shard_map.51 = (f32[512,128]{1,0:T(8,128)}, f32[2]{0:T(128)}) custom-call(f32[16,32,128]{2,1,0:T(8,128)S(1)} %get-tuple-element.6.home, f32[2,128]{1,0:T(2,128)S(1)} %get-tuple-element.7.total_ref), custom_call_target="tpu_custom_call" | custom-call | tf_op jit(solution)/shard_map/pallas_call | solution.py:392

commit v3 on v2

--- a/solution.py
+++ b/solution.py
@@ -200,13 +200,13 @@
         tail = jnp.where(from_other, halo[t], recv[t, rows:rows + 1, :])
         return jnp.concatenate([recv[t, 0:rows, :], jnp.broadcast_to(tail, (TAIL, LANES))], axis=0)
 
-    def below(v):
-        turned = pltpu.roll(v, 1, 1)
-        return jnp.where(lane == 0, pltpu.roll(turned, 1, 0), turned)
-
-    def above(v):
-        turned = pltpu.roll(v, LANES - 1, 1)
-        return jnp.where(lane == LANES - 1, pltpu.roll(turned, field[0] - 1, 0), turned)
+    def below(v, by=1):
+        turned = pltpu.roll(v, by, 1)
+        return jnp.where(lane < by, pltpu.roll(turned, 1, 0), turned)
+
+    def above(v, by=1):
+        turned = pltpu.roll(v, LANES - by, 1)
+        return jnp.where(lane >= LANES - by, pltpu.roll(turned, field[0] - 1, 0), turned)
 
     own.wait()
     all_of(recv, groups - 1, recv_sem.at[0])
@@ -221,21 +221,36 @@
     b = jnp.ones(field, jnp.float32)
     u = jnp.where(outside, 0.0, b)
 
-    def forward(t, u):
-        return emission_of(t) * (staying * u + rising * below(u) + falling * above(u))
-
-    def backward(s, b):
+    def forward_two(t, u):
+        e = emission_of(t)
+        low, low2, high, high2 = below(u), below(u, 2), above(u), above(u, 2)
+        first = e * (staying * u + rising * low + falling * high)
+        first_low = below(e) * (staying * low + rising * low2 + falling * u)
+        first_high = above(e) * (staying * high + rising * u + falling * high2)
+        return first, emission_of(t + 1) * (staying * first + rising * first_low + falling * first_high)
+
+    def backward_two(s, b):
         g = emission_of(s + 1) * b
-        return staying * g + rising * above(g) + falling * below(g)
+        low, low2, high, high2 = below(g), below(g, 2), above(g), above(g, 2)
+        first = staying * g + rising * high + falling * low
+        if s == 0:
+            return first, None
+        e = emission_of(s)
+        first_low = below(e) * (staying * low + rising * g + falling * low2)
+        first_high = above(e) * (staying * high + rising * high2 + falling * g)
+        return first, staying * (e * first) + rising * first_high + falling * first_low
 
     half = groups // 2
-    for step in range(half):
-        u = forward(step, u)
-        work[step] = u[:rows]
-        if step > 0:
-            b = backward(last - step, b)
-        work[last - step] = b[:rows]
-    b = backward(half - 1, b)
+    work[last] = b[:rows]
+    for step in range(0, half, 2):
+        first, u = forward_two(step, u)
+        work[step] = first[:rows]
+        if step + 1 < half - 1:
+            work[step + 1] = u[:rows]
+        first, b = backward_two(last - 1 - step, b)
+        work[last - 1 - step] = first[:rows]
+        if step + 1 < half - 1:
+            work[last - 2 - step] = b[:rows]
     middle = u[:rows] * b[:rows]
     work[half - 1] = middle
     part[...] = jnp.sum(middle, axis=0, keepdims=True)
@@ -256,12 +271,14 @@
     x_ring = (lambda k: across_x(k)[1], xi * 2 + core, 2 * xs, x_send, x_recv)
     spread(part, part_in, *y_ring)
 
-    for step in range(half, groups):
-        u = forward(step, u)
-        work[step] = u[:rows] * work[step]
-        if step > half:
-            b = backward(last - step, b)
-            work[last - step] = work[last - step] * b[:rows]
+    for step in range(half, groups, 2):
+        first, u = forward_two(step, u)
+        work[step] = first[:rows] * work[step]
+        work[step + 1] = u[:rows] * work[step + 1]
+        first, b = backward_two(last - 1 - step, b)
+        work[last - 1 - step] = work[last - 1 - step] * first[:rows]
+        if b is not None:
+            work[last - 2 - step] = work[last - 2 - step] * b[:rows]
 
     def back_copy(k):
         to = member(k)

time: 37.9 us -> 37.7 us (level)
  no operation moved by 1% of the time
where the time goes in v3:
time: 37.7 us; the launch traced here: 37.6 us
  Pallas kernels  36.9 us (98%)
  between operations  0.64 us (2%)
    pallas_call x1, Pallas kernels, body(): pl.pallas_call(functools.partial(kernel, groups, freqs, zs, bins), out_sh...  36.1 us
    pallas_call x1, Pallas kernels, body(): pl.pallas_call(functools.partial(finish, bins), out_shape=(jax.ShapeDtype...  0.79 us

profile of v3, /device:TPU:1, one launch (start us, length us, event | category | flops | bytes accessed | tf_op | source)
XLA Modules:
  0.0 37.6 jit_solution(10285413955354154711)
XLA Ops:
  0.6 36.1 %shard_map.50 = (f32[16,32,128]{2,1,0:T(8,128)S(1)}, f32[2,128]{1,0:T(2,128)S(1)}) custom-call(bf16[512,128]{1,0:T(8,128)(2,1)} %bitcast.11, f32[3,64]{1,0:T(4,128)} %bitcast.12, s32[2]{0:T(128)} %ids_hbm.1), custom_call_target="tpu_custom_call" | custom-call | tf_op jit(solution)/shard_map/pallas_call | solution.py:373
  36.8 0.8 %shard_map.51 = (f32[512,128]{1,0:T(8,128)}, f32[2]{0:T(128)}) custom-call(f32[16,32,128]{2,1,0:T(8,128)S(1)} %get-tuple-element.6.home, f32[2,128]{1,0:T(2,128)S(1)} %get-tuple-element.7.total_ref), custom_call_target="tpu_custom_call" | custom-call | tf_op jit(solution)/shard_map/pallas_call | solution.py:409

commit v4 on v2

--- a/solution.py
+++ b/solution.py
@@ -166,23 +166,25 @@
 
     for c in (0, 1):
         relay_copy(stage, relay, 0, c).start()
-    for k in direct:
+    for k in direct[:len(direct) // 2]:
         out_copy(k).start()
-
-    @pl.when(has_prev)
-    def _():
-        halo_pass(0)
-
-    @pl.when(has_next)
-    def _():
-        halo_pass(1)
 
     own = pltpu.make_async_copy(stage.at[tm], recv.at[tm], own_sem.at[0])
     own.start()
+
+    @pl.when(has_prev)
+    def _():
+        halo_pass(0)
+
+    @pl.when(has_next)
+    def _():
+        halo_pass(1)
 
     for c in (0, 1):
         relay_copy(stage, relay, 0, c).wait_recv()
         pass_copy(relay, recv, recv_sem, 0, c).start()
+    for k in direct[len(direct) // 2:]:
+        out_copy(k).start()
 
     loads[1].wait()
     loads[2].wait()
@@ -276,11 +278,11 @@
 
     z_part[...] = gather(part, part_in, *y_ring)
     spread(z_part, z_in, *z_ring)
-    for k in direct[len(direct) // 2:]:
-        back_copy(k).start()
     for c in (0, 1):
         relay_copy(work, relay_back, 1, c).wait_recv()
         pass_copy(relay_back, home, back_recv, 1, c).start()
+    for k in direct[len(direct) // 2:]:
+        back_copy(k).start()
     all_of(stage, groups - 1, send_sem.at[0])
     all_of(relay, 2, pass_send.at[0])
 

time: 37.9 us -> 38.5 us (1.016)
  Pallas kernels: 37.1 us -> 37.8 us
    pallas_call x1, Pallas kernels: 36.3 us -> 37 us  [body(): pl.pallas_call(functools.partial(kernel, groups, freqs, zs, bins), out_sh...]
where the time goes in v4:
time: 38.5 us; the launch traced here: 38.4 us
  Pallas kernels  37.8 us (98%)
  between operations  0.64 us (2%)
    pallas_call x1, Pallas kernels, body(): pl.pallas_call(functools.partial(kernel, groups, freqs, zs, bins), out_sh...  37 us
    pallas_call x1, Pallas kernels, body(): pl.pallas_call(functools.partial(finish, bins), out_shape=(jax.ShapeDtype...  0.79 us

profile of v4, /device:TPU:1, one launch (start us, length us, event | category | flops | bytes accessed | tf_op | source)
XLA Modules:
  0.0 38.4 jit_solution(10391738276942489461)
XLA Ops:
  0.6 37.0 %shard_map.50 = (f32[16,32,128]{2,1,0:T(8,128)S(1)}, f32[2,128]{1,0:T(2,128)S(1)}) custom-call(bf16[512,128]{1,0:T(8,128)(2,1)} %bitcast.11, f32[3,64]{1,0:T(4,128)} %bitcast.12, s32[2]{0:T(128)} %ids_hbm.1), custom_call_target="tpu_custom_call" | custom-call | tf_op jit(solution)/shard_map/pallas_call | solution.py:358
  37.6 0.8 %shard_map.51 = (f32[512,128]{1,0:T(8,128)}, f32[2]{0:T(128)}) custom-call(f32[16,32,128]{2,1,0:T(8,128)S(1)} %get-tuple-element.6.home, f32[2,128]{1,0:T(2,128)S(1)} %get-tuple-element.7.total_ref), custom_call_target="tpu_custom_call" | custom-call | tf_op jit(solution)/shard_map/pallas_call | solution.py:394

commit v5 on v2

--- a/solution.py
+++ b/solution.py
@@ -22,10 +22,9 @@
 
 def kernel(groups, freqs, zs, bins, x_hbm, w_hbm, ids_hbm, home, total_ref,
            x_half, x_full, w_ref, ids_ref, stage, recv, halo, edge, beside, work,
-           part, part_in, z_part, z_in, x_part, x_in, relay, relay_back,
+           part, part_in, z_part, z_in, x_part, x_in,
            load_sem, send_sem, recv_sem, edge_send, edge_recv, halo_send, halo_recv, back_send, back_recv,
-           part_send, part_recv, z_send, z_recv, x_send, x_recv, own_sem,
-           relay_recv, pass_send):
+           part_send, part_recv, z_send, z_recv, x_send, x_recv, own_sem):
     xs = freqs // zs
     chips = groups // 2
     tm = lax.axis_index("tm")
@@ -149,24 +148,7 @@
     def _():
         edge_copy(1, prev_fq).start()
 
-    far = chips // 2
-    near = far // 2
-    direct = [k for k in order if k[0] != far]
-
-    def relay_copy(src, dst, phase, c):
-        way = near if c == 0 else -near
-        return remote(src.at[member((far, lax.rem(core + c, 2)))], dst.at[c],
-                      (send_sem, back_send)[phase].at[0], relay_recv.at[phase, c], (member((way, 0)), fq))
-
-    def pass_copy(src, dst, r_sem, phase, c):
-        way = near if c == 0 else -near
-        origin = member((-way, 0))
-        return remote(src.at[c], dst.at[origin], pass_send.at[phase], r_sem.at[0],
-                      (member((way, lax.rem(core + c, 2))), fq))
-
-    for c in (0, 1):
-        relay_copy(stage, relay, 0, c).start()
-    for k in direct:
+    for k in order:
         out_copy(k).start()
 
     @pl.when(has_prev)
@@ -179,10 +161,6 @@
 
     own = pltpu.make_async_copy(stage.at[tm], recv.at[tm], own_sem.at[0])
     own.start()
-
-    for c in (0, 1):
-        relay_copy(stage, relay, 0, c).wait_recv()
-        pass_copy(relay, recv, recv_sem, 0, c).start()
 
     loads[1].wait()
     loads[2].wait()
@@ -269,20 +247,14 @@
 
     own_back = pltpu.make_async_copy(work.at[tm], home.at[tm], own_sem.at[1])
     own_back.start()
-    for c in (0, 1):
-        relay_copy(work, relay_back, 1, c).start()
-    for k in direct[:len(direct) // 2]:
+    for k in order[:len(order) // 2]:
         back_copy(k).start()
 
     z_part[...] = gather(part, part_in, *y_ring)
     spread(z_part, z_in, *z_ring)
-    for k in direct[len(direct) // 2:]:
+    for k in order[len(order) // 2:]:
         back_copy(k).start()
-    for c in (0, 1):
-        relay_copy(work, relay_back, 1, c).wait_recv()
-        pass_copy(relay_back, home, back_recv, 1, c).start()
     all_of(stage, groups - 1, send_sem.at[0])
-    all_of(relay, 2, pass_send.at[0])
 
     x_part[...] = gather(z_part, z_in, *z_ring)
     spread(x_part, x_in, *x_ring)
@@ -316,7 +288,6 @@
     all_of(home, groups - 1, back_recv.at[0])
     all_of(x_in, 2 * xs - 1, x_send.at[0])
     all_of(work, groups - 1, back_send.at[0])
-    all_of(relay_back, 2, pass_send.at[1])
 
 
 def finish(bins, home, total_ref, out_hbm, level_hbm, out, level, sems):
@@ -378,11 +349,8 @@
             pltpu.VMEM((zs, 1, LANES), f32),
             pltpu.VMEM((1, LANES), f32),
             pltpu.VMEM((2 * xs, 1, LANES), f32),
-            pltpu.VMEM((2, rows + 1, LANES), f32),
-            pltpu.VMEM((2, rows, LANES), f32),
             dma((3,)), dma((1,)), dma((1,)), dma((2,)), dma((2,)), dma((2, 2)), dma((1,)), dma((1,)), dma((1,)),
             dma((1,)), dma((1,)), dma((1,)), dma((1,)), dma((1,)), dma((1,)), dma((2,)),
-            dma((2, 2)), dma((2,)),
         ],
         compiler_params=pltpu.CompilerParams(
             collective_id=0, has_side_effects=True, vmem_limit_bytes=32 * 1024 * 1024

time: 37.9 us -> 37.7 us (level)
  no operation moved by 1% of the time
where the time goes in v5:
time: 37.7 us; the launch traced here: 37.6 us
  Pallas kernels  36.9 us (98%)
  between operations  0.64 us (2%)
    pallas_call x1, Pallas kernels, body(): pl.pallas_call(functools.partial(kernel, groups, freqs, zs, bins), out_sh...  36.1 us
    pallas_call x1, Pallas kernels, body(): pl.pallas_call(functools.partial(finish, bins), out_shape=(jax.ShapeDtype...  0.79 us

profile of v5, /device:TPU:1, one launch (start us, length us, event | category | flops | bytes accessed | tf_op | source)
XLA Modules:
  0.0 37.6 jit_solution(18316263645843364618)
XLA Ops:
  0.6 36.1 %shard_map.50 = (f32[16,32,128]{2,1,0:T(8,128)S(1)}, f32[2,128]{1,0:T(2,128)S(1)}) custom-call(bf16[512,128]{1,0:T(8,128)(2,1)} %bitcast.11, f32[3,64]{1,0:T(4,128)} %bitcast.12, s32[2]{0:T(128)} %ids_hbm.1), custom_call_target="tpu_custom_call" | custom-call | tf_op jit(solution)/shard_map/pallas_call | solution.py:327
  36.8 0.8 %shard_map.51 = (f32[512,128]{1,0:T(8,128)}, f32[2]{0:T(128)}) custom-call(f32[16,32,128]{2,1,0:T(8,128)S(1)} %get-tuple-element.6.home, f32[2,128]{1,0:T(2,128)S(1)} %get-tuple-element.7.total_ref), custom_call_target="tpu_custom_call" | custom-call | tf_op jit(solution)/shard_map/pallas_call | solution.py:360

commit v6 on v5

--- a/solution.py
+++ b/solution.py
@@ -207,12 +207,18 @@
         return staying * g + rising * above(g) + falling * below(g)
 
     half = groups // 2
-    for step in range(half):
+
+    def early(step, fields):
+        u, b = fields
         u = forward(step, u)
+        b = backward(last - 1 - step, b)
         work[step] = u[:rows]
-        if step > 0:
-            b = backward(last - step, b)
-        work[last - step] = b[:rows]
+        work[last - 1 - step] = b[:rows]
+        return u, b
+
+    work[last] = b[:rows]
+    u, b = lax.fori_loop(0, half - 1, early, (u, b))
+    u = forward(half - 1, u)
     b = backward(half - 1, b)
     middle = u[:rows] * b[:rows]
     work[half - 1] = middle
@@ -234,12 +240,16 @@
     x_ring = (lambda k: across_x(k)[1], xi * 2 + core, 2 * xs, x_send, x_recv)
     spread(part, part_in, *y_ring)
 
-    for step in range(half, groups):
+    def late(step, fields):
+        u, b = fields
         u = forward(step, u)
+        b = backward(last - 1 - step, b)
         work[step] = u[:rows] * work[step]
-        if step > half:
-            b = backward(last - step, b)
-            work[last - step] = work[last - step] * b[:rows]
+        work[last - 1 - step] = work[last - 1 - step] * b[:rows]
+        return u, b
+
+    u, _ = lax.fori_loop(half, last, late, (u, b))
+    work[last] = forward(last, u)[:rows] * work[last]
 
     def back_copy(k):
         to = member(k)

time: 37.7 us -> 37.1 us (0.984)
  Pallas kernels: 36.9 us -> 36.3 us
    pallas_call x1, Pallas kernels: 36.1 us -> 35.5 us  [body(): pl.pallas_call(functools.partial(kernel, groups, freqs, zs, bins), out_sh...]
where the time goes in v6:
time: 37.1 us; the launch traced here: 37 us
  Pallas kernels  36.3 us (98%)
  between operations  0.64 us (2%)
    pallas_call x1, Pallas kernels, body(): pl.pallas_call(functools.partial(kernel, groups, freqs, zs, bins), out_sh...  35.5 us
    pallas_call x1, Pallas kernels, body(): pl.pallas_call(functools.partial(finish, bins), out_shape=(jax.ShapeDtype...  0.79 us

profile of v6, /device:TPU:1, one launch (start us, length us, event | category | flops | bytes accessed | tf_op | source)
XLA Modules:
  0.0 37.0 jit_solution(12906837618955748919)
XLA Ops:
  0.6 35.5 %shard_map.50 = (f32[16,32,128]{2,1,0:T(8,128)S(1)}, f32[2,128]{1,0:T(2,128)S(1)}) custom-call(bf16[512,128]{1,0:T(8,128)(2,1)} %bitcast.11, f32[3,64]{1,0:T(4,128)} %bitcast.12, s32[2]{0:T(128)} %ids_hbm.1), custom_call_target="tpu_custom_call" | custom-call | tf_op jit(solution)/shard_map/pallas_call | solution.py:337
  36.2 0.8 %shard_map.51 = (f32[512,128]{1,0:T(8,128)}, f32[2]{0:T(128)}) custom-call(f32[16,32,128]{2,1,0:T(8,128)S(1)} %get-tuple-element.6.home, f32[2,128]{1,0:T(2,128)S(1)} %get-tuple-element.7.total_ref), custom_call_target="tpu_custom_call" | custom-call | tf_op jit(solution)/shard_map/pallas_call | solution.py:370

commit v7 on v6

--- a/solution.py
+++ b/solution.py
@@ -18,6 +18,10 @@
     for d in range(chips // 2 - 1, 0, -1):
         steps += [-d, d]
     return [(d, c) for d in steps for c in (0, 1)] + [(0, 1)]
+
+
+def loop(count, step):
+    lax.fori_loop(0, count, lambda i, c: (step(i), c)[1], 0)
 
 
 def kernel(groups, freqs, zs, bins, x_hbm, w_hbm, ids_hbm, home, total_ref,
@@ -78,19 +82,24 @@
         greet(tm, prev_fq)
 
     loads[0].wait()
-    for r in range(0, all_rows, 16):
-        x_full[r:r + 16, :] = x_half[r:r + 16, :].astype(jnp.float32)
     low_lanes = lax.broadcasted_iota(jnp.int32, (1, LANES), 1) < LANES // 2
-    nothing = jnp.zeros((1, LANES), jnp.float32)
-    for o in range(chips):
+
+    def widen(o):
+        block = pl.ds(pl.multiple_of(o * 2 * rows, 2 * rows), 2 * rows)
+        x_full[block, :] = x_half[block, :].astype(jnp.float32)
+
+    def stage_one(o):
         for p in range(2):
-            first = 2 * o * rows + p
+            first = o * 2 * rows + p
             for r in range(0, rows, 8):
                 stage[2 * o + p, r:r + 8, :] = x_full[pl.ds(first + 2 * r, 8, stride=2), :]
-            after = first + 2 * rows
-            high = x_full[after:after + 1, :] if o < chips - 1 else nothing
-            low = x_full[first - 2:first - 1, :] if o > 0 else nothing
-            stage[2 * o + p, rows:rows + 1, :] = jnp.where(low_lanes, high, low)
+            high = x_full[pl.ds(jnp.minimum(first + 2 * rows, all_rows - 2 + p), 1), :]
+            low = x_full[pl.ds(jnp.maximum(first - 2, p), 1), :]
+            stage[2 * o + p, rows:rows + 1, :] = jnp.where(
+                low_lanes, jnp.where(o < chips - 1, high, 0.0), jnp.where(o > 0, low, 0.0))
+
+    loop(chips, widen)
+    loop(chips, stage_one)
     for p in range(2):
         edge[0, p] = x_full[all_rows - 2 + p:all_rows - 1 + p, :]
         edge[1, p] = x_full[p:p + 1, :]
@@ -304,22 +313,22 @@
     groups, rows = home.shape[0], home.shape[1]
     totals = [total_ref[p:p + 1, :] for p in range(2)]
     scales = [bins / total for total in totals]
-    blocks = groups // 2
-    copies = []
-    for o in range(blocks):
-        first = o * 2 * rows
+
+    def hand_out(o):
+        first = pl.multiple_of(o * 2 * rows, 2 * rows)
         for p in range(2):
             for r in range(0, rows, 8):
                 out[pl.ds(first + p + 2 * r, 8, stride=2), :] = home[2 * o + p, r:r + 8, :] * scales[p]
         block = pl.ds(first, 2 * rows)
-        copies.append(pltpu.make_async_copy(out.at[block, :], out_hbm.at[block, :], sems.at[o]))
-        copies[-1].start()
+        pltpu.make_async_copy(out.at[block, :], out_hbm.at[block, :], sems.at[0]).start()
+
+    loop(groups // 2, hand_out)
     for p in range(2):
         level[p] = (jnp.log(totals[p] * (1.0 / bins)) * (1.0 / groups))[0, 0]
-    copies.append(pltpu.make_async_copy(level, level_hbm, sems.at[blocks]))
-    copies[-1].start()
-    for copy in copies:
-        copy.wait()
+    level_copy = pltpu.make_async_copy(level, level_hbm, sems.at[1])
+    level_copy.start()
+    pltpu.make_async_copy(out, out_hbm, sems.at[0]).wait()
+    level_copy.wait()
 
 
 def body(bins, groups, freqs, zs, emission, step_weights, template_ids):
@@ -375,7 +384,7 @@
         ),
         in_specs=[vmem, vmem],
         out_specs=(anywhere, anywhere),
-        scratch_shapes=[pltpu.VMEM((all_rows, LANES), f32), pltpu.SMEM((templates,), f32), dma((groups // 2 + 1,))],
+        scratch_shapes=[pltpu.VMEM((all_rows, LANES), f32), pltpu.SMEM((templates,), f32), dma((2,))],
         compiler_params=pltpu.CompilerParams(vmem_limit_bytes=4 * 1024 * 1024),
     )(home, total)
     posterior = post.reshape(total_rows, templates, LANES).transpose(1, 0, 2).reshape(1, templates, here)

time: 37.1 us -> 37 us (level)
  no operation moved by 1% of the time
where the time goes in v7:
time: 37 us; the launch traced here: 36.9 us
  Pallas kernels  36.3 us (98%)
  between operations  0.64 us (2%)
    pallas_call x1, Pallas kernels, body(): pl.pallas_call(functools.partial(kernel, groups, freqs, zs, bins), out_sh...  35.5 us

profile of v7, /device:TPU:1, one launch (start us, length us, event | category | flops | bytes accessed | tf_op | source)
XLA Modules:
  0.0 36.9 jit_solution(10527481586547340412)
XLA Ops:
  0.6 35.5 %shard_map.50 = (f32[16,32,128]{2,1,0:T(8,128)S(1)}, f32[2,128]{1,0:T(2,128)S(1)}) custom-call(bf16[512,128]{1,0:T(8,128)(2,1)} %bitcast.11, f32[3,64]{1,0:T(4,128)} %bitcast.12, s32[2]{0:T(128)} %ids_hbm.1), custom_call_target="tpu_custom_call" | custom-call | tf_op jit(solution)/shard_map/pallas_call | solution.py:346
  36.2 0.7 %shard_map.51 = (f32[512,128]{1,0:T(8,128)}, f32[2]{0:T(128)}) custom-call(f32[16,32,128]{2,1,0:T(8,128)S(1)} %get-tuple-element.6.home, f32[2,128]{1,0:T(2,128)S(1)} %get-tuple-element.7.total_ref), custom_call_target="tpu_custom_call" | custom-call | tf_op jit(solution)/shard_map/pallas_call | solution.py:379

commit v8 on v7

--- a/solution.py
+++ b/solution.py
@@ -237,12 +237,14 @@
         for k in range(1, count):
             remote(src, dst.at[mine], s_sem.at[0], r_sem.at[0], to_of(k)).start()
 
+    def tree_sum(values):
+        while len(values) > 1:
+            values = [sum(values[i:i + 2]) for i in range(0, len(values), 2)]
+        return values[0]
+
     def gather(src, dst, to_of, mine, count, s_sem, r_sem):
+        dst[mine] = src[...]
         all_of(dst, count - 1, r_sem.at[0])
-        value = src[...]
-        for k in range(1, count):
-            value = value + dst[lax.rem(mine + k, count)]
-        return value
 
     y_ring = (lambda k: (lax.rem(yi + k, chips) * 2 + core, fq), yi, chips, part_send, part_recv)
     z_ring = (lambda k: (tm, xi * zs + lax.rem(zi + k, zs)), zi, zs, z_send, z_recv)
@@ -269,13 +271,15 @@
     for k in order[:len(order) // 2]:
         back_copy(k).start()
 
-    z_part[...] = gather(part, part_in, *y_ring)
+    gather(part, part_in, *y_ring)
+    z_part[...] = tree_sum([part_in[i] for i in range(chips)])
     spread(z_part, z_in, *z_ring)
     for k in order[len(order) // 2:]:
         back_copy(k).start()
     all_of(stage, groups - 1, send_sem.at[0])
 
-    x_part[...] = gather(z_part, z_in, *z_ring)
+    gather(z_part, z_in, *z_ring)
+    x_part[...] = tree_sum([z_in[i] for i in range(zs)])
     spread(x_part, x_in, *x_ring)
 
     @pl.when(has_next)
@@ -290,17 +294,9 @@
 
     all_of(part_in, chips - 1, part_send.at[0])
     all_of(z_in, zs - 1, z_send.at[0])
-    all_of(x_in, 2 * xs - 1, x_recv.at[0])
-    same = x_part[...]
-    other = jnp.zeros_like(same)
-    for k in range(1, 2 * xs):
-        place, _ = across_x(k)
-        if k % 2 == 0:
-            same = same + x_in[place]
-        else:
-            other = other + x_in[place]
+    gather(x_part, x_in, *x_ring)
     for p in range(2):
-        whole = jnp.sum(jnp.where(core == p, same, other), axis=1, keepdims=True)
+        whole = jnp.sum(tree_sum([x_in[2 * i + p] for i in range(xs)]), axis=1, keepdims=True)
         total_ref[p:p + 1, :] = jnp.broadcast_to(whole, (1, LANES))
 
     own_back.wait()

time: 37 us -> 37 us (level)
  no operation moved by 1% of the time
where the time goes in v8:
time: 37 us; the launch traced here: 36.9 us
  Pallas kernels  36.2 us (98%)
  between operations  0.64 us (2%)
    pallas_call x1, Pallas kernels, body(): pl.pallas_call(functools.partial(kernel, groups, freqs, zs, bins), out_sh...  35.5 us

profile of v8, /device:TPU:1, one launch (start us, length us, event | category | flops | bytes accessed | tf_op | source)
XLA Modules:
  0.0 36.9 jit_solution(7978024434421769108)
XLA Ops:
  0.6 35.5 %shard_map.50 = (f32[16,32,128]{2,1,0:T(8,128)S(1)}, f32[2,128]{1,0:T(2,128)S(1)}) custom-call(bf16[512,128]{1,0:T(8,128)(2,1)} %bitcast.11, f32[3,64]{1,0:T(4,128)} %bitcast.12, s32[2]{0:T(128)} %ids_hbm.1), custom_call_target="tpu_custom_call" | custom-call | tf_op jit(solution)/shard_map/pallas_call | solution.py:342
  36.2 0.7 %shard_map.51 = (f32[512,128]{1,0:T(8,128)}, f32[2]{0:T(128)}) custom-call(f32[16,32,128]{2,1,0:T(8,128)S(1)} %get-tuple-element.6.home, f32[2,128]{1,0:T(2,128)S(1)} %get-tuple-element.7.total_ref), custom_call_target="tpu_custom_call" | custom-call | tf_op jit(solution)/shard_map/pallas_call | solution.py:375

commit v9 on v8

--- a/solution.py
+++ b/solution.py
@@ -11,6 +11,7 @@
 Z_CHIPS = 8
 LANES = 128
 TAIL = 8
+SPARE = 8
 
 
 def ring_order(chips):
@@ -29,6 +30,7 @@
            part, part_in, z_part, z_in, x_part, x_in,
            load_sem, send_sem, recv_sem, edge_send, edge_recv, halo_send, halo_recv, back_send, back_recv,
            part_send, part_recv, z_send, z_recv, x_send, x_recv, own_sem):
+    part, z_part, x_part = part.at[0], z_part.at[0], x_part.at[0]
     xs = freqs // zs
     chips = groups // 2
     tm = lax.axis_index("tm")
@@ -343,7 +345,7 @@
         functools.partial(kernel, groups, freqs, zs, bins),
         out_shape=(
             jax.ShapeDtypeStruct((groups, rows, LANES), f32),
-            jax.ShapeDtypeStruct((templates, LANES), f32),
+            jax.ShapeDtypeStruct((TAIL, LANES), f32),
         ),
         in_specs=[hbm, hbm, hbm],
         out_specs=(vmem, vmem),
@@ -354,16 +356,16 @@
             pltpu.SMEM(template_ids.shape, jnp.int32),
             pltpu.VMEM((groups, rows + 1, LANES), f32),
             pltpu.VMEM((groups, rows + 1, LANES), f32),
-            pltpu.VMEM((groups, 1, LANES), f32),
-            pltpu.VMEM((2, 2, 1, LANES), f32),
-            pltpu.VMEM((2, 2, 1, LANES), f32),
+            pltpu.VMEM((groups + SPARE, 1, LANES), f32),
+            pltpu.VMEM((2 + SPARE, 2, 1, LANES), f32),
+            pltpu.VMEM((2 + SPARE, 2, 1, LANES), f32),
             pltpu.VMEM((groups, rows, LANES), f32),
-            pltpu.VMEM((1, LANES), f32),
-            pltpu.VMEM((groups // 2, 1, LANES), f32),
-            pltpu.VMEM((1, LANES), f32),
-            pltpu.VMEM((zs, 1, LANES), f32),
-            pltpu.VMEM((1, LANES), f32),
-            pltpu.VMEM((2 * xs, 1, LANES), f32),
+            pltpu.VMEM((1 + SPARE, 1, LANES), f32),
+            pltpu.VMEM((groups // 2 + SPARE, 1, LANES), f32),
+            pltpu.VMEM((1 + SPARE, 1, LANES), f32),
+            pltpu.VMEM((zs + SPARE, 1, LANES), f32),
+            pltpu.VMEM((1 + SPARE, 1, LANES), f32),
+            pltpu.VMEM((2 * xs + SPARE, 1, LANES), f32),
             dma((3,)), dma((1,)), dma((1,)), dma((2,)), dma((2,)), dma((2, 2)), dma((1,)), dma((1,)), dma((1,)),
             dma((1,)), dma((1,)), dma((1,)), dma((1,)), dma((1,)), dma((1,)), dma((2,)),
         ],

time: 37 us -> 37 us (level)
  no operation moved by 1% of the time
where the time goes in v9:
time: 37 us; the launch traced here: 36.9 us
  Pallas kernels  36.2 us (98%)
  between operations  0.64 us (2%)
    pallas_call x1, Pallas kernels, body(): pl.pallas_call(functools.partial(kernel, groups, freqs, zs, bins), out_sh...  35.5 us

profile of v9, /device:TPU:1, one launch (start us, length us, event | category | flops | bytes accessed | tf_op | source)
XLA Modules:
  0.0 36.9 jit_solution(16711062588624783381)
XLA Ops:
  0.6 35.5 %shard_map.50 = (f32[16,32,128]{2,1,0:T(8,128)S(1)}, f32[8,128]{1,0:T(8,128)S(1)}) custom-call(bf16[512,128]{1,0:T(8,128)(2,1)} %bitcast.11, f32[3,64]{1,0:T(4,128)} %bitcast.12, s32[2]{0:T(128)} %ids_hbm.1), custom_call_target="tpu_custom_call" | custom-call | tf_op jit(solution)/shard_map/pallas_call | solution.py:344
  36.2 0.7 %shard_map.51 = (f32[512,128]{1,0:T(8,128)}, f32[2]{0:T(128)}) custom-call(f32[16,32,128]{2,1,0:T(8,128)S(1)} %get-tuple-element.6.home, f32[8,128]{1,0:T(8,128)S(1)} %get-tuple-element.7.total_ref), custom_call_target="tpu_custom_call" | custom-call | tf_op jit(solution)/shard_map/pallas_call | solution.py:377
